TPU v7x, 256 devices: a whole 4x4x8 slice. The times are simulated.
256 devices in a mesh: seq: 32 (over x, z), dp: 8 (over y, core).
Axes of the slice: x: 4, y: 4, z: 8, core: 2. Of those that a mesh axis runs over, the one named last changes fastest.
Arguments:
- hidden_in: bfloat16 [8, 4096, 4096], P('dp', 'seq'), may hold values from -6 to 6
- queries: bfloat16 [8, 4096, 4096], P('dp', 'seq'), may hold values from -12 to 12, as said below
- keys: bfloat16 [8, 4096, 1024], P('dp', 'seq'), may hold values from -9 to 9, as said below
- values: bfloat16 [8, 4096, 1024], P('dp', 'seq'), may hold values from -6 to 6
- attn_out: bfloat16 [8, 4096, 4096], P('dp', 'seq'), may hold values from -6 to 6
- out_grad: bfloat16 [8, 4096, 4096], P('dp', 'seq'), may hold values from -1.1953125 to 1.1953125
- log_totals: float32 [8, 4096, 32], P('dp', 'seq')
Outputs:
- query_grad: bfloat16 [8, 4096, 4096], P('dp', 'seq')
- key_grad: bfloat16 [8, 4096, 1024], P('dp', 'seq')
- value_grad: bfloat16 [8, 4096, 1024], P('dp', 'seq')
- weight_grad: float32 [4096, 1024], P(('seq', 'dp'))
Inputs may be any that keep to these rules, and one draw needn't show every extreme that they name: queries drawn independently. keys drawn independently.
All inputs are finite; a program needn't handle non-finite values.
Results may differ from a plain program's by a relative error of at most 0.0049.
Values may be sent and summed in bfloat16 or wider, within the bound.
A program may use at most 192 MiB of HBM per device.

v0:
```python
import jax
import jax.numpy as jnp
from jax import lax
from jax.sharding import PartitionSpec as P

HEADS = 32
KV_HEADS = 8
HEAD_DIM = 128
DOCS = 2


def head_backward(query_head, key_head, value_head, grad_head, total_column, delta_column):
    length = query_head.shape[0]
    doc_len = length // DOCS
    block = min(512, doc_len)
    score_scale = HEAD_DIM ** (-0.5)
    query_rows = []
    key_rows = []
    value_rows = []
    for trajectory in range(DOCS):
        base_row = trajectory * doc_len
        key_accum = jnp.zeros((doc_len, HEAD_DIM), jnp.float32)
        value_accum = jnp.zeros((doc_len, HEAD_DIM), jnp.float32)
        for position in range(doc_len // block):
            start_row = base_row + position * block
            end_row = start_row + block
            local_end = end_row - base_row
            query_block = query_head[start_row:end_row]
            grad_block = grad_head[start_row:end_row]
            key_front = key_head[base_row:end_row]
            value_front = value_head[base_row:end_row]
            scores = (
                lax.dot_general(
                    query_block,
                    key_front,
                    (((1,), (1,)), ((), ())),
                    preferred_element_type=jnp.float32,
                )
                * score_scale
            )
            causal = (position * block + jnp.arange(block))[:, None] >= jnp.arange(local_end)[
                None, :
            ]
            probs = jnp.where(causal, jnp.exp(scores - total_column[start_row:end_row, None]), 0.0)
            probs_low = probs.astype(jnp.bfloat16)
            value_step = lax.dot_general(
                probs_low, grad_block, (((0,), (0,)), ((), ())), preferred_element_type=jnp.float32
            )
            dprobs = lax.dot_general(
                grad_block,
                value_front,
                (((1,), (1,)), ((), ())),
                preferred_element_type=jnp.float32,
            )
            dscores = probs * (dprobs - delta_column[start_row:end_row, None])
            dscores_low = dscores.astype(jnp.bfloat16)
            query_rows.append(
                (
                    jnp.dot(dscores_low, key_front, preferred_element_type=jnp.float32)
                    * score_scale
                ).astype(jnp.bfloat16)
            )
            key_step = (
                lax.dot_general(
                    dscores_low,
                    query_block,
                    (((0,), (0,)), ((), ())),
                    preferred_element_type=jnp.float32,
                )
                * score_scale
            )
            if local_end == doc_len:
                key_accum = key_accum + key_step
                value_accum = value_accum + value_step
            else:
                key_accum = key_accum.at[:local_end].add(key_step)
                value_accum = value_accum.at[:local_end].add(value_step)
        key_rows.append(key_accum)
        value_rows.append(value_accum)
    return (
        jnp.concatenate(query_rows, axis=0),
        jnp.concatenate(key_rows, axis=0),
        jnp.concatenate(value_rows, axis=0),
    )


def body(hidden_in, queries, keys, values, attn_out, out_grad, log_totals):
    tokens_here = queries.shape[1]
    devices_seq = lax.axis_size("seq")
    heads_here = HEADS // devices_seq
    groups = HEADS // KV_HEADS
    query_local = queries[0]
    grad_local = out_grad[0]
    totals_local = log_totals[0]
    query_heads, grad_heads, output_heads = (
        lax.all_to_all(query_local, "seq", split_axis=1, concat_axis=0, tiled=True),
        lax.all_to_all(grad_local, "seq", split_axis=1, concat_axis=0, tiled=True),
        lax.all_to_all(attn_out[0], "seq", split_axis=1, concat_axis=0, tiled=True),
    )
    total_heads = lax.all_to_all(totals_local, "seq", split_axis=1, concat_axis=0, tiled=True)
    length = query_heads.shape[0]
    delta_heads = jnp.sum(
        (grad_heads.astype(jnp.float32) * output_heads.astype(jnp.float32)).reshape(
            length, heads_here, HEAD_DIM
        ),
        axis=2,
    )
    key_copies = jnp.broadcast_to(
        keys[0].reshape(tokens_here, KV_HEADS, 1, HEAD_DIM),
        (tokens_here, KV_HEADS, groups, HEAD_DIM),
    ).reshape(tokens_here, HEADS * HEAD_DIM)
    value_copies = jnp.broadcast_to(
        values[0].reshape(tokens_here, KV_HEADS, 1, HEAD_DIM),
        (tokens_here, KV_HEADS, groups, HEAD_DIM),
    ).reshape(tokens_here, HEADS * HEAD_DIM)
    key_shared, value_shared = (
        lax.all_to_all(key_copies, "seq", split_axis=1, concat_axis=0, tiled=True),
        lax.all_to_all(value_copies, "seq", split_axis=1, concat_axis=0, tiled=True),
    )
    query_part, key_part, value_part = head_backward(
        query_heads, key_shared, value_shared, grad_heads, total_heads[:, 0], delta_heads[:, 0]
    )
    query_grad = lax.all_to_all(query_part, "seq", split_axis=0, concat_axis=1, tiled=True)
    key_terms, value_terms = (
        lax.all_to_all(key_part, "seq", split_axis=0, concat_axis=1, tiled=True),
        lax.all_to_all(value_part, "seq", split_axis=0, concat_axis=1, tiled=True),
    )
    key_grad = (
        jnp.sum(key_terms.reshape(tokens_here, KV_HEADS, groups, HEAD_DIM), axis=2)
        .reshape(tokens_here, KV_HEADS * HEAD_DIM)
        .astype(jnp.bfloat16)
    )
    value_grad = (
        jnp.sum(value_terms.reshape(tokens_here, KV_HEADS, groups, HEAD_DIM), axis=2)
        .reshape(tokens_here, KV_HEADS * HEAD_DIM)
        .astype(jnp.bfloat16)
    )
    hidden_local = hidden_in[0]
    weight_grad = lax.psum_scatter(
        lax.dot_general(
            hidden_local, value_grad, (((0,), (0,)), ((), ())), preferred_element_type=jnp.float32
        ),
        ("seq", "dp"),
        scatter_dimension=0,
        tiled=True,
    )
    return (query_grad[None], key_grad[None], value_grad[None], weight_grad)


def solution(mesh):
    placed = (
        P("dp", "seq", None),
        P("dp", "seq", None),
        P("dp", "seq", None),
        P("dp", "seq", None),
        P("dp", "seq", None),
        P("dp", "seq", None),
        P("dp", "seq", None),
    )
    return jax.shard_map(
        body,
        mesh=mesh,
        in_specs=placed,
        out_specs=(
            P("dp", "seq", None),
            P("dp", "seq", None),
            P("dp", "seq", None),
            P(("seq", "dp"), None),
        ),
        check_vma=False,
    )
```

profile of v0, /device:TPU:1, one launch (start us, length us, event | category | flops | bytes accessed | tf_op | source)
XLA Modules:
  0.0 1544.4 jit_solution(1575198051245969990)
XLA Ops:
  7.2 12.0 all-to-all-start.2
  20.2 7.5 all-to-all-done.2
  29.0 3.9 all-to-all-start.1
  32.9 2.3 copy.63
  35.2 22.1 %all-to-all-done.1 = bf16[128,32,128]{2,0,1:T(8,128)(2,1)S(1)} async-done(((bf16[128,32,128]{2,0,1:T(8,128)(2,1)}), bf16[128,32,128]{2,0,1:T(8,128)(2,1)S(1)}, u32[]{:S(2)}, u32[]{:S(2)}) %all-to-all-start.1) | async-done | bytes 1048608 | tf_op jit(solution)/shard_map/all_to_all | solution.py:117
  57.3 8.2 all-to-all-start
  65.5 2.3 copy.66
  67.8 22.2 %all-to-all-done = bf16[128,32,128]{0,2,1:T(8,128)(2,1)S(1)} async-done(((bf16[128,32,128]{0,2,1:T(8,128)(2,1)}), bf16[128,32,128]{0,2,1:T(8,128)(2,1)S(1)}, u32[]{:S(2)}, u32[]{:S(2)}) %all-to-all-start) | async-done | bytes 1048608 | tf_op jit(solution)/shard_map/all_to_all | solution.py:96
  91.0 8.2 all-to-all-start.3
  101.7 2.2 fusion.65
  104.9 1.7 copy.80
  106.6 1.7 copy.78
  108.3 1.7 copy.76
  109.9 1.7 copy.74
  111.6 1.7 copy.72
  117.8 5.8 all-to-all-done.3
  143.7 2.0 copy-done.2
  146.5 54.9 %all_to_all.141 = f32[32,128,128]{2,1,0:T(8,128)S(1)} all-to-all(f32[32,128,128]{2,1,0:T(8,128)S(1)} %bitcast.181), channel_id=1, replica_groups=mesh['seq'=32,'dp'=8] {'seq'}, dimensions={0} | all-to-all | bytes 4194304 | tf_op jit(solution)/shard_map/all_to_all | solution.py:126
  201.7 8.1 convolution_bitcast_fusion
  209.8 17.4 %copy.91 = f32[4096,1024]{1,0:T(8,128)} copy(f32[4096,1024]{0,1:T(8,128)} %convolution_bitcast_fusion) | data formatting | bytes 33554432
  229.7 8.2 all-to-all-start.5
  238.0 24.6 %all-to-all-done.5 = bf16[128,32,128]{0,2,1:T(8,128)(2,1)S(1)} async-done(((bf16[128,32,128]{0,2,1:T(8,128)(2,1)}), bf16[128,32,128]{0,2,1:T(8,128)(2,1)S(1)}, u32[]{:S(2)}, u32[]{:S(2)}) %all-to-all-start.5) | async-done | bytes 1048608 | tf_op jit(solution)/shard_map/all_to_all | solution.py:98
  263.9 9.4 all-to-all-start.4
  275.5 22.0 %all-to-all-done.4 = bf16[128,32,128]{2,0,1:T(8,128)(2,1)S(1)} async-done(((bf16[128,32,128]{2,0,1:T(8,128)(2,1)}), bf16[128,32,128]{2,0,1:T(8,128)(2,1)S(1)}, u32[]{:S(2)}, u32[]{:S(2)}) %all-to-all-start.4) | async-done | bytes 1048608 | tf_op jit(solution)/shard_map/all_to_all | solution.py:118
  319.9 9.7 all-to-all-start.6
  331.1 1.8 fusion.38
  339.7 13.1 all-to-all-done.6
  352.8 9.7 all-to-all-start.7
  362.5 2.9 copy.84
  365.4 2.4 broadcast_in_dim.38
  367.8 41.9 %all-to-all-done.7 = f32[32,128,128]{2,1,0:T(8,128)S(1)} async-done(((f32[32,128,128]{2,1,0:T(8,128)}), f32[32,128,128]{2,1,0:T(8,128)S(1)}, u32[]{:S(2)}, u32[]{:S(2)}) %all-to-all-start.7) | async-done | bytes 2097184 | tf_op jit(solution)/shard_map/all_to_all | solution.py:125
  413.3 1124.2 %reduce-scatter.4.cloned.1.call-done = f32[16,1024]{1,0:T(8,128)} async-done(((f32[4096,1024]{1,0:T(8,128)}), f32[16,1024]{1,0:T(8,128)}) %reduce-scatter.4.cloned.1.call-update) | async-done | bytes 65552
  (251 shorter events, 72.2 us)
Async XLA Ops:
  7.2 194.5 %copy-start = (bf16[1,128,4096]{2,1,0:T(8,128)(2,1)S(1)}, bf16[1,128,4096]{2,1,0:T(8,128)(2,1)}, u32[]{:S(2)}) copy-start(bf16[1,128,4096]{2,1,0:T(8,128)(2,1)} %param.31) | copy-start | bytes 3145732
  7.2 20.6 %all-to-all-start.2 = ((f32[128,32,1]{0,2,1:T(1,128)}), f32[128,32,1]{0,2,1:T(1,128)S(1)}, u32[]{:S(2)}, u32[]{:S(2)}) async-start(f32[128,32,1]{0,2,1:T(1,128)} %bitcast.250), calls=%async_computation.2 | async-start | bytes 32768 | tf_op jit(solution)/shard_map/all_to_all | solution.py:100
  29.0 28.3 %all-to-all-start.1 = ((bf16[128,32,128]{2,0,1:T(8,128)(2,1)}), bf16[128,32,128]{2,0,1:T(8,128)(2,1)S(1)}, u32[]{:S(2)}, u32[]{:S(2)}) async-start(bf16[128,32,128]{2,0,1:T(8,128)(2,1)} %bitcast.3), calls=%async_computation.1 | async-start | bytes 2097152 | tf_op jit(solution)/shard_map/all_to_all | solution.py:117
  57.3 32.7 %all-to-all-start = ((bf16[128,32,128]{0,2,1:T(8,128)(2,1)}), bf16[128,32,128]{0,2,1:T(8,128)(2,1)S(1)}, u32[]{:S(2)}, u32[]{:S(2)}) async-start(bf16[128,32,128]{0,2,1:T(8,128)(2,1)} %bitcast.184), calls=%async_computation | async-start | bytes 2097152 | tf_op jit(solution)/shard_map/all_to_all | solution.py:96
  91.0 32.6 %all-to-all-start.3 = ((bf16[128,32,128]{0,2,1:T(8,128)(2,1)}), bf16[128,32,128]{0,2,1:T(8,128)(2,1)S(1)}, u32[]{:S(2)}, u32[]{:S(2)}) async-start(bf16[128,32,128]{0,2,1:T(8,128)(2,1)} %bitcast.182), calls=%async_computation.3 | async-start | bytes 2097152 | tf_op jit(solution)/shard_map/all_to_all | solution.py:97
  99.1 1438.4 %reduce-scatter.4.cloned.1.call-start = ((), (), s32[]{:S(2)}) async-start(), calls=%async_computation.10 | async-start | bytes 16842752
  104.9 37.4 %copy-start.46 = (bf16[4,128,128]{2,1,0:T(8,128)(2,1)}, bf16[4,128,128]{2,1,0:T(8,128)(2,1)S(1)}, u32[]{:S(2)}) copy-start(bf16[4,128,128]{2,1,0:T(8,128)(2,1)S(1)} %copy.82) | copy-start | bytes 393220
  114.2 10.7 copy-start.57
  124.0 13.3 copy-start.31
  124.1 7.8 copy-start.33
  124.3 3.6 copy-start.43
  124.4 15.9 %copy-start.35 = (bf16[4,128,128]{2,1,0:T(8,128)(2,1)}, bf16[4,128,128]{2,1,0:T(8,128)(2,1)S(1)}, u32[]{:S(2)}) copy-start(bf16[4,128,128]{2,1,0:T(8,128)(2,1)S(1)} %copy.75) | copy-start | bytes 393220
  124.6 9.9 copy-start.37
  124.7 5.2 copy-start.39
  124.9 3.0 copy-start.41
  228.4 9.5 copy-start.70
  229.7 32.9 %all-to-all-start.5 = ((bf16[128,32,128]{0,2,1:T(8,128)(2,1)}), bf16[128,32,128]{0,2,1:T(8,128)(2,1)S(1)}, u32[]{:S(2)}, u32[]{:S(2)}) async-start(bf16[128,32,128]{0,2,1:T(8,128)(2,1)} %bitcast.15), calls=%async_computation.5 | async-start | bytes 2097152 | tf_op jit(solution)/shard_map/all_to_all | solution.py:98
  263.9 33.6 %copy-start.28 = (f32[512,512]{1,0:T(8,128)S(1)}, f32[512,512]{1,0:T(8,128)}, u32[]{:S(2)}) copy-start(f32[512,512]{1,0:T(8,128)} %copy-done.27) | copy-start | bytes 3145732
  263.9 33.6 %all-to-all-start.4 = ((bf16[128,32,128]{2,0,1:T(8,128)(2,1)}), bf16[128,32,128]{2,0,1:T(8,128)(2,1)S(1)}, u32[]{:S(2)}, u32[]{:S(2)}) async-start(bf16[128,32,128]{2,0,1:T(8,128)(2,1)} %bitcast.12), calls=%async_computation.4 | async-start | bytes 2097152 | tf_op jit(solution)/shard_map/all_to_all | solution.py:118
  274.9 23.9 %copy-start.59 = (bf16[4,128,128]{2,1,0:T(8,128)(2,1)S(1)}, bf16[4,128,128]{2,1,0:T(8,128)(2,1)}, u32[]{:S(2)}) copy-start(bf16[4,128,128]{2,1,0:T(8,128)(2,1)} %copy.76) | copy-start | bytes 393220
  304.5 2.9 copy-start.5
  308.5 2.9 copy-start.14
  308.5 2.4 copy-start.11
  308.5 2.4 copy-start.34
  313.2 2.9 copy-start.3
  318.1 11.4 copy-start.23
  319.9 11.3 copy-start.53
  319.9 32.9 %all-to-all-start.6 = ((bf16[32,128,128]{2,1,0:T(8,128)(2,1)}), bf16[32,128,128]{2,1,0:T(8,128)(2,1)}, u32[]{:S(2)}, u32[]{:S(2)}) async-start(bf16[32,128,128]{2,1,0:T(8,128)(2,1)} %bitcast.207), calls=%async_computation.6 | async-start | bytes 2097152 | tf_op jit(solution)/shard_map/all_to_all | solution.py:123
  329.5 3.4 copy-start.19
  329.6 3.4 copy-start.55
  352.8 56.9 %all-to-all-start.7 = ((f32[32,128,128]{2,1,0:T(8,128)}), f32[32,128,128]{2,1,0:T(8,128)S(1)}, u32[]{:S(2)}, u32[]{:S(2)}) async-start(f32[32,128,128]{2,1,0:T(8,128)} %bitcast.62), calls=%async_computation.7 | async-start | bytes 4194304 | tf_op jit(solution)/shard_map/all_to_all | solution.py:125
  365.4 1172.2 %copy-start.1 = (bf16[1,128,4096]{2,1,0:T(8,128)(2,1)S(1)}, bf16[1,128,4096]{2,1,0:T(8,128)(2,1)}, u32[]{:S(2)}) copy-start(bf16[1,128,4096]{2,1,0:T(8,128)(2,1)} %param.31) | copy-start | bytes 3145732
  (60 other events, 89.7 us)
Sparse Core Ops, SparseCore 0:
  227.4 1310.1 reduce-scatter.3
where the time goes:
time: 1550 us; the launch traced here: 1540 us
  waiting for transfers between devices  1280 us (83%)
  local copies, waits for them, and re-layouts  77.7 us (5%)
  starting transfers between devices  69.4 us (4%)
  blocking collectives  54.9 us (4%)
  matrix products  37.9 us (2%)
    unnamed x2, waiting for transfers between devices  1120 us
    all_to_all x1, blocking collectives, body(): lax.all_to_all(value_part, 'seq', split_axis=0, concat_axis=1, tiled=True)  54.9 us
    unnamed x174, local copies, waits for them, and re-layouts  49.7 us
    all_to_all x1, waiting for transfers between devices, body(): lax.all_to_all(key_part, 'seq', split_axis=0, concat_axis=1, tiled=True)  41.9 us
  transfers between devices with their start and end apart: 9, of which 9 were waited for; matrix products, arithmetic and copies ran while one was open for 4% of the time, Pallas kernels for 0%

commit v1 on v0

v1 whole, which is shorter than its diff:
```python
import functools

import jax
import jax.numpy as jnp
from jax import lax
from jax.experimental import pallas as pl
from jax.experimental.pallas import tpu as pltpu
from jax.sharding import PartitionSpec as P

HEADS = 32
KV_HEADS = 8
HEAD_DIM = 128
DOCS = 2
SCALE = HEAD_DIM ** (-0.5)
LOG2E = 1.4426950408889634
ROWS = 128
UNITS = 16
NT = (((1,), (1,)), ((), ()))
TN = (((0,), (0,)), ((), ()))
NN = (((1,), (0,)), ((), ()))
MESH = pl.DeviceIdType.MESH
ANY = pl.BlockSpec(memory_space=pl.ANY)
VMEM = pl.BlockSpec(memory_space=pltpu.VMEM)
DMA = pltpu.SemaphoreType.DMA


def place():
    seq = lax.axis_index("seq")
    unit = lax.rem(seq, UNITS)
    return seq, seq - unit, unit, unit // 8, lax.rem(unit, 8)


def send(src, dst, send_sem, recv_sem, **device):
    copy = pltpu.make_async_remote_copy(
        src_ref=src,
        dst_ref=dst,
        send_sem=send_sem,
        recv_sem=recv_sem,
        device_id=device,
        device_id_type=MESH,
    )
    copy.start()


def drain(ref, sem):
    pltpu.make_async_copy(ref, ref, sem).wait()


def rows_of(block):
    return pl.ds(pl.multiple_of(block * ROWS, ROWS), ROWS)


def columns_of(block, width=HEAD_DIM):
    return pl.ds(pl.multiple_of(block * width, width), width)


def exchange_kernel(
    query_ref,
    grad_ref,
    key_ref,
    value_ref,
    small_ref,
    hidden_ref,
    query_unit,
    grad_unit,
    key_unit,
    value_unit,
    small_unit,
    hidden_unit,
    own_sem,
    ring_send,
    ring_recv,
    pass_send,
    pass_recv,
    bulk_send,
    bulk_recv,
):
    seq, base, unit, half, lane = place()
    dp = lax.axis_index("dp")
    barrier = pltpu.get_barrier_semaphore()
    for step in range(1, UNITS):
        pl.semaphore_signal(
            barrier,
            inc=1,
            device_id={"seq": base + lax.rem(unit + step, UNITS)},
            device_id_type=MESH,
        )
    for step in range(1, 8):
        pl.semaphore_signal(
            barrier, inc=1, device_id={"dp": lax.rem(dp + step, 8)}, device_id_type=MESH
        )
    pl.semaphore_wait(barrier, 22)

    partner = base + (1 - half) * 8 + lane
    pairs = ((key_ref, key_unit), (value_ref, value_unit))
    for step in range(1, 8):
        target = lax.rem(lane + step, 8)
        for which, (source, landing) in enumerate(pairs):
            send(
                source.at[:, columns_of(target)],
                landing.at[rows_of(unit)],
                ring_send.at[which],
                ring_recv.at[which, lane],
                seq=base + half * 8 + target,
            )
    for which, (source, landing) in enumerate(pairs):
        send(
            source.at[:, columns_of(lane)],
            landing.at[rows_of(unit)],
            pass_send.at[which],
            pass_recv.at[which],
            seq=partner,
        )
    for step in range(1, UNITS):
        target = lax.rem(unit + step, UNITS)
        heads = lax.rem(target, 8) * 2 + target // 8
        send(
            query_ref.at[:, columns_of(heads, 256)],
            query_unit.at[rows_of(unit)],
            bulk_send.at[0],
            bulk_recv.at[0],
            seq=base + target,
        )
        send(
            grad_ref.at[:, columns_of(heads, 256)],
            grad_unit.at[rows_of(unit)],
            bulk_send.at[1],
            bulk_recv.at[1],
            seq=base + target,
        )
        send(
            small_ref.at[target],
            small_unit.at[unit],
            bulk_send.at[2],
            bulk_recv.at[2],
            seq=base + target,
        )
    for step in range(1, 8):
        target = lax.rem(dp + step, 8)
        send(
            hidden_ref.at[:, columns_of(target, 512)],
            hidden_unit.at[dp],
            bulk_send.at[3],
            bulk_recv.at[3],
            dp=target,
        )
    mine = lane * 2 + half
    own = (
        (key_ref.at[:, columns_of(lane)], key_unit.at[rows_of(unit)]),
        (value_ref.at[:, columns_of(lane)], value_unit.at[rows_of(unit)]),
        (query_ref.at[:, columns_of(mine, 256)], query_unit.at[rows_of(unit)]),
        (grad_ref.at[:, columns_of(mine, 256)], grad_unit.at[rows_of(unit)]),
        (small_ref.at[unit], small_unit.at[unit]),
        (hidden_ref.at[:, columns_of(dp, 512)], hidden_unit.at[dp]),
    )
    own = [pltpu.make_async_copy(*pair, own_sem.at[i]) for i, pair in enumerate(own)]
    for copy in own:
        copy.start()
    for step in range(1, 8):
        source = lax.rem(lane - step + 8, 8)
        for which, (_, landing) in enumerate(pairs):
            block = landing.at[rows_of(half * 8 + source)]
            drain(block, ring_recv.at[which, source])
            send(block, block, pass_send.at[which], pass_recv.at[which], seq=partner)
    for copy in own:
        copy.wait()
    for which, (_, landing) in enumerate(pairs):
        drain(landing.at[pl.ds(0, 7 * ROWS)], ring_send.at[which])
        drain(landing.at[pl.ds(0, 8 * ROWS)], pass_send.at[which])
        drain(landing.at[pl.ds(0, 8 * ROWS)], pass_recv.at[which])
    landings = (
        query_unit.at[pl.ds(0, 15 * ROWS)],
        grad_unit.at[pl.ds(0, 15 * ROWS)],
        small_unit.at[pl.ds(0, 15)],
        hidden_unit.at[pl.ds(0, 7)],
    )
    for i, landing in enumerate(landings):
        drain(landing, bulk_send.at[i])
        drain(landing, bulk_recv.at[i])


def exchange(queries, out_grad, keys, values, small, hidden):
    low = jnp.bfloat16
    return pl.pallas_call(
        exchange_kernel,
        out_shape=(
            jax.ShapeDtypeStruct((UNITS * ROWS, 256), low),
            jax.ShapeDtypeStruct((UNITS * ROWS, 256), low),
            jax.ShapeDtypeStruct((UNITS * ROWS, HEAD_DIM), low),
            jax.ShapeDtypeStruct((UNITS * ROWS, HEAD_DIM), low),
            jax.ShapeDtypeStruct((UNITS, 8, ROWS), jnp.float32),
            jax.ShapeDtypeStruct((8, ROWS, 512), low),
        ),
        in_specs=[ANY] * 6,
        out_specs=(ANY,) * 6,
        scratch_shapes=[
            DMA((6,)),
            DMA((2,)),
            DMA((2, 8)),
            DMA((2,)),
            DMA((2,)),
            DMA((4,)),
            DMA((4,)),
        ],
        compiler_params=pltpu.CompilerParams(collective_id=0, has_side_effects=True),
        name="exchange",
    )(queries, out_grad, keys, values, small, hidden)


def attention_kernel(
    query_ref,
    grad_ref,
    key_ref,
    value_ref,
    small_ref,
    query_out,
    key_out,
    value_out,
    key_low,
    value_low,
):
    block = 512
    per = block // ROWS
    key_out[...] = jnp.zeros_like(key_out)
    value_out[...] = jnp.zeros_like(value_out)
    causal = lax.broadcasted_iota(jnp.int32, (block, block), 0) <= lax.broadcasted_iota(
        jnp.int32, (block, block), 1
    )
    for position in range(query_ref.shape[0] // block):
        rows = slice(position * block, (position + 1) * block)
        for head in range(2):
            columns = slice(head * HEAD_DIM, (head + 1) * HEAD_DIM)
            query = query_ref[rows, columns]
            grad = grad_ref[rows, columns]
            total = jnp.concatenate(
                [small_ref[position * per + t, head : head + 1, :] for t in range(per)], axis=1
            )
            delta = jnp.concatenate(
                [small_ref[position * per + t, head + 2 : head + 3, :] for t in range(per)], axis=1
            )
            total = total * LOG2E
            query_sum = None
            for front in range(position + 1):
                fronts = slice(front * block, (front + 1) * block)
                key = key_ref[fronts, :]
                value = value_ref[fronts, :]
                scores = lax.dot_general(key, query, NT, preferred_element_type=jnp.float32)
                probs = jnp.exp2(scores * (SCALE * LOG2E) - total)
                if front == position:
                    probs = jnp.where(causal, probs, 0.0)
                dprobs = lax.dot_general(value, grad, NT, preferred_element_type=jnp.float32)
                value_out[fronts, :] += lax.dot_general(
                    probs.astype(jnp.bfloat16), grad, NN, preferred_element_type=jnp.float32
                )
                dscores = (probs * (dprobs - delta)).astype(jnp.bfloat16)
                key_out[fronts, :] += lax.dot_general(
                    dscores, query, NN, preferred_element_type=jnp.float32
                )
                step = lax.dot_general(dscores, key, TN, preferred_element_type=jnp.float32)
                query_sum = step if query_sum is None else query_sum + step
            query_out[rows, columns] = (query_sum * SCALE).astype(jnp.bfloat16)
    key_sum = key_out[...] * SCALE
    key_out[...] = key_sum
    key_low[...] = key_sum.astype(jnp.bfloat16)
    value_low[...] = value_out[...].astype(jnp.bfloat16)


def attention(query, grad, key, value, small):
    length = query.shape[0]
    narrow = (length, HEAD_DIM)
    return pl.pallas_call(
        attention_kernel,
        out_shape=(
            jax.ShapeDtypeStruct((length, 256), jnp.bfloat16),
            jax.ShapeDtypeStruct(narrow, jnp.float32),
            jax.ShapeDtypeStruct(narrow, jnp.float32),
            jax.ShapeDtypeStruct(narrow, jnp.bfloat16),
            jax.ShapeDtypeStruct(narrow, jnp.bfloat16),
        ),
        in_specs=[VMEM] * 5,
        out_specs=(VMEM,) * 5,
        compiler_params=pltpu.CompilerParams(vmem_limit_bytes=48 * 1024 * 1024),
        name="attention",
    )(query, grad, key, value, small)


def return_kernel(
    query_part,
    key_part,
    value_part,
    key_low,
    value_low,
    hidden_ref,
    query_grad,
    key_grad,
    value_grad,
    weight_grad,
    kept,
    halves,
    staged,
    gathered,
    product,
    product_in,
    summed,
    final_in,
    own_sem,
    kept_sem,
    half_send,
    half_recv,
    ring_send,
    ring_recv,
    query_send,
    query_recv,
    gather_send,
    gather_recv,
    core_send,
    core_recv,
    cross_send,
    cross_recv,
    final_send,
    final_recv,
):
    seq, base, unit, half, lane = place()
    dp = lax.axis_index("dp")
    across = seq // 8
    core = lax.rem(dp, 2)
    twin = dp + 1 - 2 * core
    owner = 4 * dp + across
    keeps = (owner == seq).astype(jnp.int32)
    barrier = pltpu.get_barrier_semaphore()
    for step in range(1, UNITS):
        pl.semaphore_signal(
            barrier,
            inc=1,
            device_id={"seq": base + lax.rem(unit + step, UNITS)},
            device_id_type=MESH,
        )
    for step in range(1, 4):
        pl.semaphore_signal(
            barrier,
            inc=1,
            device_id={"seq": lax.rem(across + step, 4) * 8 + lane},
            device_id_type=MESH,
        )
        pl.semaphore_signal(
            barrier, inc=1, device_id={"dp": lax.rem(dp + 2 * step, 8)}, device_id_type=MESH
        )
    pl.semaphore_signal(barrier, inc=1, device_id={"dp": twin}, device_id_type=MESH)
    for step in range(8):
        sender = lax.rem(seq, 4) * 8 + step
        outside = jnp.logical_or(sender != seq, seq // 4 != dp)

        @pl.when(outside)
        def _():
            pl.semaphore_signal(
                barrier,
                inc=1,
                device_id={"seq": sender, "dp": seq // 4},
                device_id_type=MESH,
            )

    pl.semaphore_wait(barrier, 30 - keeps)

    partner = base + (1 - half) * 8 + lane
    parts = ((value_part, value_low), (key_part, key_low))
    for which, (wide, low) in enumerate(parts):
        pltpu.make_async_copy(
            wide.at[pl.ds(pl.multiple_of(half * 8 * ROWS, ROWS), 8 * ROWS)],
            kept.at[which],
            kept_sem.at[which],
        ).start()
        for step in range(8):
            target = lax.rem(lane + 1 + step, 8)
            send(
                low.at[rows_of((1 - half) * 8 + target)],
                halves.at[which, target],
                half_send.at[which],
                half_recv.at[which, target],
                seq=partner,
            )
    for which in range(2):
        drain(kept.at[which], kept_sem.at[which])
        for step in range(8):
            target = lax.rem(lane + 1 + step, 8)
            drain(halves.at[which, target], half_recv.at[which, target])
            staged[which, target] = (
                kept[which, rows_of(target)] + halves[which, target].astype(jnp.float32)
            ).astype(jnp.bfloat16)
            landing = (gathered.at[dp] if which == 0 else key_grad).at[:, columns_of(lane)]
            if step < 7:
                send(
                    staged.at[which, target],
                    landing,
                    ring_send.at[which],
                    ring_recv.at[which],
                    seq=base + half * 8 + target,
                )
            else:
                pltpu.make_async_copy(staged.at[which, target], landing, own_sem.at[which]).start()
        if which == 0:
            mine = columns_of(lane * 2 + half, 256)
            for step in range(1, UNITS):
                target = lax.rem(unit + step, UNITS)
                send(
                    query_part.at[rows_of(target)],
                    query_grad.at[:, mine],
                    query_send,
                    query_recv,
                    seq=base + target,
                )
            pltpu.make_async_copy(
                query_part.at[rows_of(unit)], query_grad.at[:, mine], own_sem.at[2]
            ).start()

    drain(staged.at[0, 0], own_sem.at[0])
    drain(staged.at[0, pl.ds(0, 7)], ring_recv.at[0])
    block = gathered.at[dp]
    for step in (2, 1, 3):
        send(
            block,
            block,
            gather_send,
            gather_recv.at[dp // 2],
            dp=lax.rem(dp + 2 * step, 8),
        )
    send(block, block, core_send, core_recv, dp=twin)
    pltpu.make_async_copy(block, value_grad, own_sem.at[3]).start()
    for step in (1, 3, 2):
        source = lax.rem(dp + 2 * step, 8)
        arrived = gathered.at[source]
        drain(arrived, gather_recv.at[source // 2])
        send(arrived, arrived, core_send, core_recv, dp=twin)
    drain(gathered.at[pl.ds(0, 4)], core_recv)

    for step in range(4):
        target = lax.rem(across + 1 + step, 4)
        total = None
        for source in range(8):
            term = lax.dot_general(
                hidden_ref[source, :, columns_of(target)],
                gathered[source],
                TN,
                preferred_element_type=jnp.float32,
            )
            total = term if total is None else total + term
        if step < 3:
            product[target] = total.astype(jnp.bfloat16)
            send(
                product.at[target],
                product_in.at[across],
                cross_send,
                cross_recv,
                seq=target * 8 + lane,
            )
        else:
            summed[...] = total
    drain(product.at[pl.ds(0, 3)], cross_recv)
    for step in range(1, 4):
        summed[...] += product_in[lax.rem(across + step, 4)].astype(jnp.float32)
    for step in range(8):
        target = lax.rem(dp + step, 8)
        piece = summed.at[pl.ds(pl.multiple_of(target * 16, 16), 16)]
        landing = final_in.at[lane]
        if step == 0:

            @pl.when(keeps == 0)
            def _():
                send(
                    piece, landing, final_send.at[step], final_recv.at[lane], seq=owner, dp=target
                )

            @pl.when(keeps == 1)
            def _():
                pltpu.make_async_copy(piece, landing, final_recv.at[lane]).start()

        else:
            send(piece, landing, final_send.at[step], final_recv.at[lane], seq=owner, dp=target)
    for step in range(8):
        drain(final_in.at[step], final_recv.at[step])
        if step < 7:
            drain(final_in.at[step], final_send.at[step + 1])

    @pl.when(keeps == 0)
    def _():
        drain(final_in.at[0], final_send.at[0])

    total = final_in[0]
    for step in range(1, 8):
        total = total + final_in[step]
    weight_grad[...] = total

    drain(staged.at[1, 0], own_sem.at[1])
    drain(query_part.at[rows_of(0)], own_sem.at[2])
    drain(gathered.at[0], own_sem.at[3])
    drain(staged.at[1, pl.ds(0, 7)], ring_recv.at[1])
    drain(query_part.at[pl.ds(0, 15 * ROWS)], query_recv)
    drain(query_part.at[pl.ds(0, 15 * ROWS)], query_send)
    for which in range(2):
        drain(halves.at[which], half_send.at[which])
        drain(staged.at[which, pl.ds(0, 7)], ring_send.at[which])
    drain(gathered.at[pl.ds(0, 3)], gather_send)
    drain(gathered.at[pl.ds(0, 4)], core_send)
    drain(product.at[pl.ds(0, 3)], cross_send)


def give_back(query_part, key_part, value_part, key_low, value_low, hidden):
    low = jnp.bfloat16
    wide = jnp.float32
    return pl.pallas_call(
        return_kernel,
        out_shape=(
            jax.ShapeDtypeStruct((ROWS, HEADS * HEAD_DIM), low),
            jax.ShapeDtypeStruct((ROWS, KV_HEADS * HEAD_DIM), low),
            jax.ShapeDtypeStruct((ROWS, KV_HEADS * HEAD_DIM), low),
            jax.ShapeDtypeStruct((16, KV_HEADS * HEAD_DIM), wide),
        ),
        in_specs=[ANY] * 5 + [VMEM],
        out_specs=(ANY, ANY, ANY, VMEM),
        scratch_shapes=[
            pltpu.VMEM((2, 8 * ROWS, HEAD_DIM), wide),
            pltpu.VMEM((2, 8, ROWS, HEAD_DIM), low),
            pltpu.VMEM((2, 8, ROWS, HEAD_DIM), low),
            pltpu.VMEM((8, ROWS, KV_HEADS * HEAD_DIM), low),
            pltpu.VMEM((4, ROWS, KV_HEADS * HEAD_DIM), low),
            pltpu.VMEM((4, ROWS, KV_HEADS * HEAD_DIM), low),
            pltpu.VMEM((ROWS, KV_HEADS * HEAD_DIM), wide),
            pltpu.VMEM((8, 16, KV_HEADS * HEAD_DIM), wide),
            DMA((4,)),
            DMA((2,)),
            DMA((2,)),
            DMA((2, 8)),
            DMA((2,)),
            DMA((2,)),
            DMA,
            DMA,
            DMA,
            DMA((4,)),
            DMA,
            DMA,
            DMA,
            DMA,
            DMA((8,)),
            DMA((8,)),
        ],
        compiler_params=pltpu.CompilerParams(
            collective_id=1, has_side_effects=True, vmem_limit_bytes=48 * 1024 * 1024
        ),
        name="give_back",
    )(query_part, key_part, value_part, key_low, value_low, hidden)


def body(hidden_in, queries, keys, values, attn_out, out_grad, log_totals):
    delta = jnp.sum(
        (out_grad[0].astype(jnp.float32) * attn_out[0].astype(jnp.float32)).reshape(
            ROWS, HEADS, HEAD_DIM
        ),
        axis=2,
    )

    def by_unit(array):
        return array.reshape(ROWS, 8, 2, 2).transpose(2, 1, 3, 0).reshape(UNITS, 2, ROWS)

    small = jnp.concatenate(
        [by_unit(log_totals[0]), by_unit(delta), jnp.zeros((UNITS, 4, ROWS), jnp.float32)], axis=1
    )
    query_unit, grad_unit, key_unit, value_unit, small_unit, hidden_unit = exchange(
        queries[0], out_grad[0], keys[0], values[0], small, hidden_in[0]
    )
    query_part, key_part, value_part, key_low, value_low = attention(
        query_unit, grad_unit, key_unit, value_unit, small_unit
    )
    query_grad, key_grad, value_grad, weight_grad = give_back(
        query_part, key_part, value_part, key_low, value_low, hidden_unit
    )
    return (query_grad[None], key_grad[None], value_grad[None], weight_grad)


def solution(mesh):
    rows = P("dp", "seq", None)
    return jax.shard_map(
        body,
        mesh=mesh,
        in_specs=(rows,) * 7,
        out_specs=(rows, rows, rows, P(("seq", "dp"), None)),
        check_vma=False,
    )
```

time: 1550 us -> 204 us (0.13)
  the two profiles are of different devices: /device:TPU:1 before, /device:TPU:23 now
where the time goes in v1:
time: 204 us
  Pallas kernels  193 us (95%)
  local copies, waits for them, and re-layouts  7.17 us (4%)
  other arithmetic  3.11 us (2%)
    pallas_call x1, Pallas kernels, give_back(): pl.pallas_call(return_kernel, out_shape=(jax.ShapeDtypeStruct((ROWS, HEAD...  110 us
    pallas_call x1, Pallas kernels, exchange(): pl.pallas_call(exchange_kernel, out_shape=(jax.ShapeDtypeStruct((UNITS *...  67.9 us
    pallas_call x1, Pallas kernels, attention(): pl.pallas_call(attention_kernel, out_shape=(jax.ShapeDtypeStruct((length,...  15.6 us
    unnamed x11, local copies, waits for them, and re-layouts  6.29 us

profile of v1, /device:TPU:23, one launch (start us, length us, event | category | flops | bytes accessed | tf_op | source)
XLA Modules:
  0.0 204.1 jit_solution(7361416973820539323)
XLA Ops:
  0.6 0.1 pad.2.clone
  0.7 0.7 copy.14
  1.4 1.8 multiply_bitcast_fusion
  3.2 0.4 copy.17
  3.6 0.6 reduce_sum.9
  4.2 0.1 copy.15
  4.3 0.7 maximum_maximum_fusion.small_ref
  5.0 67.9 %exchange.1 = (bf16[2048,256]{1,0:T(8,128)(2,1)}, bf16[2048,256]{1,0:T(8,128)(2,1)}, bf16[2048,128]{1,0:T(8,128)(2,1)}, bf16[2048,128]{1,0:T(8,128)(2,1)}, f32[1...) custom-call(bf16[128,4096]{1,0:T(8,128)(2,1)} %bitcast.25, bf16[128,4096]{1,0:T(8,128)(2,1)} %bitcast.24, ...), custom_call_target="tpu_custom_call" | custom-call | tf_op jit(solution)/shard_map/exchange/pallas_call | solution.py:184
  72.9 0.0 copy-start
  72.9 1.0 copy-done
  74.0 0.0 copy-start.1
  74.0 1.0 copy-done.1
  75.0 0.0 copy-start.2
  75.0 0.8 copy-done.2
  75.8 15.6 %attention.1 = (bf16[2048,256]{1,0:T(8,128)(2,1)S(1)}, f32[2048,128]{1,0:T(8,128)S(1)}, f32[2048,128]{1,0:T(8,128)S(1)}, bf16[2048,128]{1,0:T(8,128)(2,1)S(1)}, bf16[2048,128]{1,0:T(8,128)(2,1)S(1)}) custom-call(bf16[2048,256]{1,0:T(8,128)(2,1)} %get-tuple-element.19.query_ref, bf16[2048,256]{1,0:T(8,128)(2,1)} %get-tuple-element.20.grad_ref, ...), custom_call_target="tpu_custom_call" | custom-call | tf_op jit(solution)/shard_map/attention/pallas_call | solution.py:271
  91.4 109.7 %give_back.1 = (bf16[128,4096]{1,0:T(8,128)(2,1)S(1)}, bf16[128,1024]{1,0:T(8,128)(2,1)S(1)}, bf16[128,1024]{1,0:T(8,128)(2,1)S(1)}, f32[16,1024]{1,0:T(8,128)S(1)}) custom-call(bf16[2048,256]{1,0:T(8,128)(2,1)S(1)} %get-tuple-element.24.query_part, f32[2048,128]{1,0:T(8,128)S(1)} %get-tuple-element.25.key_part, ...), custom_call_target="tpu_custom_call" | custom-call | tf_op jit(solution)/shard_map/give_back/pallas_call | solution.py:509
  201.1 1.0 copy.22
  202.1 0.7 copy.23
  202.8 0.7 copy.24
  203.5 0.6 copy.25
  (2 shorter events, 0.0 us)
Async XLA Ops:
  72.9 1.0 copy-start
  74.0 1.0 copy-start.1
  75.0 0.8 copy-start.2

commit v2 on v1

--- a/solution.py
+++ b/solution.py
@@ -74,9 +74,13 @@
     pass_recv,
     bulk_send,
     bulk_recv,
+    core_send,
+    core_recv,
+    hidden_recv,
 ):
     seq, base, unit, half, lane = place()
     dp = lax.axis_index("dp")
+    twin = dp + 1 - 2 * lax.rem(dp, 2)
     barrier = pltpu.get_barrier_semaphore()
     for step in range(1, UNITS):
         pl.semaphore_signal(
@@ -85,11 +89,9 @@
             device_id={"seq": base + lax.rem(unit + step, UNITS)},
             device_id_type=MESH,
         )
-    for step in range(1, 8):
-        pl.semaphore_signal(
-            barrier, inc=1, device_id={"dp": lax.rem(dp + step, 8)}, device_id_type=MESH
-        )
-    pl.semaphore_wait(barrier, 22)
+    for other in (lax.rem(dp + 2, 8), lax.rem(dp + 4, 8), lax.rem(dp + 6, 8), twin):
+        pl.semaphore_signal(barrier, inc=1, device_id={"dp": other}, device_id_type=MESH)
+    pl.semaphore_wait(barrier, 19)
 
     partner = base + (1 - half) * 8 + lane
     pairs = ((key_ref, key_unit), (value_ref, value_unit))
@@ -111,6 +113,15 @@
             pass_recv.at[which],
             seq=partner,
         )
+    for step in (2, 1, 3):
+        send(
+            hidden_ref,
+            hidden_unit.at[dp],
+            bulk_send.at[3],
+            hidden_recv.at[dp // 2],
+            dp=lax.rem(dp + 2 * step, 8),
+        )
+    send(hidden_ref, hidden_unit.at[dp], core_send, core_recv, dp=twin)
     for step in range(1, UNITS):
         target = lax.rem(unit + step, UNITS)
         heads = lax.rem(target, 8) * 2 + target // 8
@@ -134,15 +145,6 @@
             bulk_send.at[2],
             bulk_recv.at[2],
             seq=base + target,
-        )
-    for step in range(1, 8):
-        target = lax.rem(dp + step, 8)
-        send(
-            hidden_ref.at[:, columns_of(target, 512)],
-            hidden_unit.at[dp],
-            bulk_send.at[3],
-            bulk_recv.at[3],
-            dp=target,
         )
     mine = lane * 2 + half
     own = (
@@ -151,7 +153,7 @@
         (query_ref.at[:, columns_of(mine, 256)], query_unit.at[rows_of(unit)]),
         (grad_ref.at[:, columns_of(mine, 256)], grad_unit.at[rows_of(unit)]),
         (small_ref.at[unit], small_unit.at[unit]),
-        (hidden_ref.at[:, columns_of(dp, 512)], hidden_unit.at[dp]),
+        (hidden_ref, hidden_unit.at[dp]),
     )
     own = [pltpu.make_async_copy(*pair, own_sem.at[i]) for i, pair in enumerate(own)]
     for copy in own:
@@ -162,6 +164,11 @@
             block = landing.at[rows_of(half * 8 + source)]
             drain(block, ring_recv.at[which, source])
             send(block, block, pass_send.at[which], pass_recv.at[which], seq=partner)
+    for step in (1, 3, 2):
+        source = lax.rem(dp + 2 * step, 8)
+        arrived = hidden_unit.at[source]
+        drain(arrived, hidden_recv.at[source // 2])
+        send(arrived, arrived, core_send, core_recv, dp=twin)
     for copy in own:
         copy.wait()
     for which, (_, landing) in enumerate(pairs):
@@ -172,11 +179,13 @@
         query_unit.at[pl.ds(0, 15 * ROWS)],
         grad_unit.at[pl.ds(0, 15 * ROWS)],
         small_unit.at[pl.ds(0, 15)],
-        hidden_unit.at[pl.ds(0, 7)],
     )
     for i, landing in enumerate(landings):
         drain(landing, bulk_send.at[i])
         drain(landing, bulk_recv.at[i])
+    drain(hidden_unit.at[pl.ds(0, 3)], bulk_send.at[3])
+    drain(hidden_unit.at[pl.ds(0, 4)], core_send)
+    drain(hidden_unit.at[pl.ds(0, 4)], core_recv)
 
 
 def exchange(queries, out_grad, keys, values, small, hidden):
@@ -189,7 +198,7 @@
             jax.ShapeDtypeStruct((UNITS * ROWS, HEAD_DIM), low),
             jax.ShapeDtypeStruct((UNITS * ROWS, HEAD_DIM), low),
             jax.ShapeDtypeStruct((UNITS, 8, ROWS), jnp.float32),
-            jax.ShapeDtypeStruct((8, ROWS, 512), low),
+            jax.ShapeDtypeStruct((8, ROWS, HEADS * HEAD_DIM), low),
         ),
         in_specs=[ANY] * 6,
         out_specs=(ANY,) * 6,
@@ -200,6 +209,9 @@
             DMA((2,)),
             DMA((2,)),
             DMA((4,)),
+            DMA((3,)),
+            DMA,
+            DMA,
             DMA((4,)),
         ],
         compiler_params=pltpu.CompilerParams(collective_id=0, has_side_effects=True),
@@ -298,13 +310,17 @@
     kept,
     halves,
     staged,
-    gathered,
+    value_own,
+    value_in,
+    hidden,
     product,
     product_in,
     summed,
+    piece,
+    piece_in,
+    final,
     final_in,
     own_sem,
-    kept_sem,
     half_send,
     half_recv,
     ring_send,
@@ -313,20 +329,16 @@
     query_recv,
     gather_send,
     gather_recv,
-    core_send,
-    core_recv,
     cross_send,
     cross_recv,
+    piece_send,
+    piece_recv,
     final_send,
     final_recv,
 ):
     seq, base, unit, half, lane = place()
     dp = lax.axis_index("dp")
     across = seq // 8
-    core = lax.rem(dp, 2)
-    twin = dp + 1 - 2 * core
-    owner = 4 * dp + across
-    keeps = (owner == seq).astype(jnp.int32)
     barrier = pltpu.get_barrier_semaphore()
     for step in range(1, UNITS):
         pl.semaphore_signal(
@@ -342,24 +354,11 @@
             device_id={"seq": lax.rem(across + step, 4) * 8 + lane},
             device_id_type=MESH,
         )
+    for step in range(1, 8):
         pl.semaphore_signal(
-            barrier, inc=1, device_id={"dp": lax.rem(dp + 2 * step, 8)}, device_id_type=MESH
-        )
-    pl.semaphore_signal(barrier, inc=1, device_id={"dp": twin}, device_id_type=MESH)
-    for step in range(8):
-        sender = lax.rem(seq, 4) * 8 + step
-        outside = jnp.logical_or(sender != seq, seq // 4 != dp)
-
-        @pl.when(outside)
-        def _():
-            pl.semaphore_signal(
-                barrier,
-                inc=1,
-                device_id={"seq": sender, "dp": seq // 4},
-                device_id_type=MESH,
-            )
-
-    pl.semaphore_wait(barrier, 30 - keeps)
+            barrier, inc=1, device_id={"dp": lax.rem(dp + step, 8)}, device_id_type=MESH
+        )
+    pl.semaphore_wait(barrier, 25)
 
     partner = base + (1 - half) * 8 + lane
     parts = ((value_part, value_low), (key_part, key_low))
@@ -367,7 +366,7 @@
         pltpu.make_async_copy(
             wide.at[pl.ds(pl.multiple_of(half * 8 * ROWS, ROWS), 8 * ROWS)],
             kept.at[which],
-            kept_sem.at[which],
+            own_sem.at[which],
         ).start()
         for step in range(8):
             target = lax.rem(lane + 1 + step, 8)
@@ -378,15 +377,16 @@
                 half_recv.at[which, target],
                 seq=partner,
             )
+    pltpu.make_async_copy(hidden_ref, hidden, own_sem.at[2]).start()
     for which in range(2):
-        drain(kept.at[which], kept_sem.at[which])
+        drain(kept.at[which], own_sem.at[which])
         for step in range(8):
             target = lax.rem(lane + 1 + step, 8)
             drain(halves.at[which, target], half_recv.at[which, target])
             staged[which, target] = (
                 kept[which, rows_of(target)] + halves[which, target].astype(jnp.float32)
             ).astype(jnp.bfloat16)
-            landing = (gathered.at[dp] if which == 0 else key_grad).at[:, columns_of(lane)]
+            landing = (value_own if which == 0 else key_grad).at[:, columns_of(lane)]
             if step < 7:
                 send(
                     staged.at[which, target],
@@ -396,7 +396,9 @@
                     seq=base + half * 8 + target,
                 )
             else:
-                pltpu.make_async_copy(staged.at[which, target], landing, own_sem.at[which]).start()
+                pltpu.make_async_copy(
+                    staged.at[which, target], landing, own_sem.at[3 + which]
+                ).start()
         if which == 0:
             mine = columns_of(lane * 2 + half, 256)
             for step in range(1, UNITS):
@@ -409,40 +411,32 @@
                     seq=base + target,
                 )
             pltpu.make_async_copy(
-                query_part.at[rows_of(unit)], query_grad.at[:, mine], own_sem.at[2]
+                query_part.at[rows_of(unit)], query_grad.at[:, mine], own_sem.at[5]
             ).start()
 
-    drain(staged.at[0, 0], own_sem.at[0])
+    drain(staged.at[0, 0], own_sem.at[3])
     drain(staged.at[0, pl.ds(0, 7)], ring_recv.at[0])
-    block = gathered.at[dp]
-    for step in (2, 1, 3):
-        send(
-            block,
-            block,
+    for step in range(1, 8):
+        target = lax.rem(dp + step, 8)
+        send(
+            value_own.at[:, columns_of(target)],
+            value_in.at[rows_of(dp)],
             gather_send,
-            gather_recv.at[dp // 2],
-            dp=lax.rem(dp + 2 * step, 8),
-        )
-    send(block, block, core_send, core_recv, dp=twin)
-    pltpu.make_async_copy(block, value_grad, own_sem.at[3]).start()
-    for step in (1, 3, 2):
-        source = lax.rem(dp + 2 * step, 8)
-        arrived = gathered.at[source]
-        drain(arrived, gather_recv.at[source // 2])
-        send(arrived, arrived, core_send, core_recv, dp=twin)
-    drain(gathered.at[pl.ds(0, 4)], core_recv)
-
+            gather_recv,
+            dp=target,
+        )
+    pltpu.make_async_copy(value_own, value_grad, own_sem.at[6]).start()
+    value_in[rows_of(dp), :] = value_own[:, columns_of(dp)]
+    drain(hidden, own_sem.at[2])
+    drain(value_in.at[pl.ds(0, 7 * ROWS)], gather_recv)
     for step in range(4):
         target = lax.rem(across + 1 + step, 4)
-        total = None
-        for source in range(8):
-            term = lax.dot_general(
-                hidden_ref[source, :, columns_of(target)],
-                gathered[source],
-                TN,
-                preferred_element_type=jnp.float32,
-            )
-            total = term if total is None else total + term
+        total = lax.dot_general(
+            value_in[...],
+            hidden[:, columns_of(target, 8 * ROWS)],
+            TN,
+            preferred_element_type=jnp.float32,
+        )
         if step < 3:
             product[target] = total.astype(jnp.bfloat16)
             send(
@@ -455,78 +449,85 @@
         else:
             summed[...] = total
     drain(product.at[pl.ds(0, 3)], cross_recv)
-    for step in range(1, 4):
-        summed[...] += product_in[lax.rem(across + step, 4)].astype(jnp.float32)
     for step in range(8):
+        target = lax.rem(lane + 1 + step, 8)
+        columns = columns_of(target)
+        total = summed[:, columns]
+        for source in range(1, 4):
+            total = total + product_in[lax.rem(across + source, 4), :, columns].astype(jnp.float32)
+        if step < 7:
+            piece[target] = total
+            send(
+                piece.at[target],
+                piece_in.at[lane],
+                piece_send,
+                piece_recv,
+                seq=across * 8 + target,
+            )
+        else:
+            piece_in[lane] = total
+    drain(piece.at[pl.ds(0, 7)], piece_recv)
+    total = piece_in[0]
+    for step in range(1, 8):
+        total = total + piece_in[step]
+    final[...] = total.T
+    for step in range(1, 8):
         target = lax.rem(dp + step, 8)
-        piece = summed.at[pl.ds(pl.multiple_of(target * 16, 16), 16)]
-        landing = final_in.at[lane]
-        if step == 0:
-
-            @pl.when(keeps == 0)
-            def _():
-                send(
-                    piece, landing, final_send.at[step], final_recv.at[lane], seq=owner, dp=target
-                )
-
-            @pl.when(keeps == 1)
-            def _():
-                pltpu.make_async_copy(piece, landing, final_recv.at[lane]).start()
-
-        else:
-            send(piece, landing, final_send.at[step], final_recv.at[lane], seq=owner, dp=target)
-    for step in range(8):
-        drain(final_in.at[step], final_recv.at[step])
-        if step < 7:
-            drain(final_in.at[step], final_send.at[step + 1])
-
-    @pl.when(keeps == 0)
-    def _():
-        drain(final_in.at[0], final_send.at[0])
-
-    total = final_in[0]
-    for step in range(1, 8):
-        total = total + final_in[step]
-    weight_grad[...] = total
-
-    drain(staged.at[1, 0], own_sem.at[1])
-    drain(query_part.at[rows_of(0)], own_sem.at[2])
-    drain(gathered.at[0], own_sem.at[3])
+        send(
+            final.at[pl.ds(pl.multiple_of(target * 16, 16), 16)],
+            final_in.at[:, columns_of(dp)],
+            final_send,
+            final_recv,
+            dp=target,
+        )
+    final_in[:, columns_of(dp)] = final[pl.ds(pl.multiple_of(dp * 16, 16), 16), :]
+    drain(final.at[pl.ds(0, 7 * 16)], final_recv)
+    weight_grad[...] = final_in[...]
+
+    drain(staged.at[1, 0], own_sem.at[4])
+    drain(query_part.at[rows_of(0)], own_sem.at[5])
+    drain(value_own, own_sem.at[6])
     drain(staged.at[1, pl.ds(0, 7)], ring_recv.at[1])
     drain(query_part.at[pl.ds(0, 15 * ROWS)], query_recv)
     drain(query_part.at[pl.ds(0, 15 * ROWS)], query_send)
     for which in range(2):
         drain(halves.at[which], half_send.at[which])
         drain(staged.at[which, pl.ds(0, 7)], ring_send.at[which])
-    drain(gathered.at[pl.ds(0, 3)], gather_send)
-    drain(gathered.at[pl.ds(0, 4)], core_send)
+    drain(value_in.at[pl.ds(0, 7 * ROWS)], gather_send)
     drain(product.at[pl.ds(0, 3)], cross_send)
+    drain(piece.at[pl.ds(0, 7)], piece_send)
+    drain(final.at[pl.ds(0, 7 * 16)], final_send)
 
 
 def give_back(query_part, key_part, value_part, key_low, value_low, hidden):
     low = jnp.bfloat16
     wide = jnp.float32
+    columns = KV_HEADS * HEAD_DIM
     return pl.pallas_call(
         return_kernel,
         out_shape=(
             jax.ShapeDtypeStruct((ROWS, HEADS * HEAD_DIM), low),
-            jax.ShapeDtypeStruct((ROWS, KV_HEADS * HEAD_DIM), low),
-            jax.ShapeDtypeStruct((ROWS, KV_HEADS * HEAD_DIM), low),
-            jax.ShapeDtypeStruct((16, KV_HEADS * HEAD_DIM), wide),
+            jax.ShapeDtypeStruct((ROWS, columns), low),
+            jax.ShapeDtypeStruct((ROWS, columns), low),
+            jax.ShapeDtypeStruct((16, columns), wide),
         ),
-        in_specs=[ANY] * 5 + [VMEM],
+        in_specs=[ANY] * 6,
         out_specs=(ANY, ANY, ANY, VMEM),
         scratch_shapes=[
             pltpu.VMEM((2, 8 * ROWS, HEAD_DIM), wide),
             pltpu.VMEM((2, 8, ROWS, HEAD_DIM), low),
             pltpu.VMEM((2, 8, ROWS, HEAD_DIM), low),
-            pltpu.VMEM((8, ROWS, KV_HEADS * HEAD_DIM), low),
-            pltpu.VMEM((4, ROWS, KV_HEADS * HEAD_DIM), low),
-            pltpu.VMEM((4, ROWS, KV_HEADS * HEAD_DIM), low),
-            pltpu.VMEM((ROWS, KV_HEADS * HEAD_DIM), wide),
-            pltpu.VMEM((8, 16, KV_HEADS * HEAD_DIM), wide),
-            DMA((4,)),
-            DMA((2,)),
+            pltpu.VMEM((ROWS, columns), low),
+            pltpu.VMEM((8 * ROWS, HEAD_DIM), low),
+            pltpu.VMEM((8 * ROWS, HEADS * HEAD_DIM), low),
+            pltpu.VMEM((4, ROWS, columns), low),
+            pltpu.VMEM((4, ROWS, columns), low),
+            pltpu.VMEM((ROWS, columns), wide),
+            pltpu.VMEM((8, ROWS, ROWS), wide),
+            pltpu.VMEM((8, ROWS, ROWS), wide),
+            pltpu.VMEM((ROWS, ROWS), wide),
+            pltpu.VMEM((16, columns), wide),
+            DMA((7,)),
             DMA((2,)),
             DMA((2, 8)),
             DMA((2,)),
@@ -534,13 +535,13 @@
             DMA,
             DMA,
             DMA,
-            DMA((4,)),
-            DMA,
-            DMA,
-            DMA,
-            DMA,
-            DMA((8,)),
-            DMA((8,)),
+            DMA,
+            DMA,
+            DMA,
+            DMA,
+            DMA,
+            DMA,
+            DMA,
         ],
         compiler_params=pltpu.CompilerParams(
             collective_id=1, has_side_effects=True, vmem_limit_bytes=48 * 1024 * 1024
@@ -570,7 +571,12 @@
         query_unit, grad_unit, key_unit, value_unit, small_unit
     )
     query_grad, key_grad, value_grad, weight_grad = give_back(
-        query_part, key_part, value_part, key_low, value_low, hidden_unit
+        query_part,
+        key_part,
+        value_part,
+        key_low,
+        value_low,
+        hidden_unit.reshape(8 * ROWS, HEADS * HEAD_DIM),
     )
     return (query_grad[None], key_grad[None], value_grad[None], weight_grad)
 

time: 204 us -> 164 us (0.80)
  the two profiles are of different devices: /device:TPU:23 before, /device:TPU:1 now
where the time goes in v2:
time: 164 us; the launch traced here: 163 us
  Pallas kernels  152 us (93%)
  local copies, waits for them, and re-layouts  7.17 us (4%)
  other arithmetic  3.11 us (2%)
    pallas_call x1, Pallas kernels, exchange(): pl.pallas_call(exchange_kernel, out_shape=(jax.ShapeDtypeStruct((UNITS *...  69.5 us
    pallas_call x1, Pallas kernels, give_back(): pl.pallas_call(return_kernel, out_shape=(jax.ShapeDtypeStruct((ROWS, HEAD...  67.3 us
    pallas_call x1, Pallas kernels, attention(): pl.pallas_call(attention_kernel, out_shape=(jax.ShapeDtypeStruct((length,...  15.6 us
    unnamed x11, local copies, waits for them, and re-layouts  6.29 us

profile of v2, /device:TPU:1, one launch (start us, length us, event | category | flops | bytes accessed | tf_op | source)
XLA Modules:
  0.0 163.4 jit_solution(17031481301695727410)
XLA Ops:
  0.6 0.1 pad.2.clone
  0.7 0.7 copy.14
  1.4 1.8 %multiply_bitcast_fusion = f32[16,8,32,128]{3,1,2,0:T(8,128)S(1)} fusion(bf16[1,128,4096]{2,1,0:T(8,128)(2,1)} %param.11, bf16[1,128,4096]{2,1,0:T(8,128)(2,1)} %param.12), kind=kLoop, calls=%fused_computation | loop fusion | flops 1572864 | bytes 4194304
  3.2 0.4 copy.17
  3.6 0.6 reduce_sum.9
  4.2 0.1 copy.15
  4.3 0.7 maximum_maximum_fusion.small_ref
  5.0 69.5 %exchange.1 = (bf16[2048,256]{1,0:T(8,128)(2,1)}, bf16[2048,256]{1,0:T(8,128)(2,1)}, bf16[2048,128]{1,0:T(8,128)(2,1)}, bf16[2048,128]{1,0:T(8,128)(2,1)}, f32[1...) custom-call(bf16[128,4096]{1,0:T(8,128)(2,1)} %bitcast.27, bf16[128,4096]{1,0:T(8,128)(2,1)} %bitcast.26, ...), custom_call_target="tpu_custom_call" | custom-call | tf_op jit(solution)/shard_map/exchange/pallas_call | solution.py:193
  74.6 0.0 copy-start
  74.6 1.0 copy-done
  75.6 0.0 copy-start.1
  75.6 1.0 copy-done.1
  76.7 0.0 copy-start.2
  76.7 0.8 copy-done.2
  77.5 15.6 %attention.1 = (bf16[2048,256]{1,0:T(8,128)(2,1)S(1)}, f32[2048,128]{1,0:T(8,128)S(1)}, f32[2048,128]{1,0:T(8,128)S(1)}, bf16[2048,128]{1,0:T(8,128)(2,1)S(1)}, bf16[2048,128]{1,0:T(8,128)(2,1)S(1)}) custom-call(bf16[2048,256]{1,0:T(8,128)(2,1)} %get-tuple-element.19.query_ref, bf16[2048,256]{1,0:T(8,128)(2,1)} %get-tuple-element.20.grad_ref, ...), custom_call_target="tpu_custom_call" | custom-call | tf_op jit(solution)/shard_map/attention/pallas_call | solution.py:283
  93.1 67.3 %give_back.1 = (bf16[128,4096]{1,0:T(8,128)(2,1)S(1)}, bf16[128,1024]{1,0:T(8,128)(2,1)S(1)}, bf16[128,1024]{1,0:T(8,128)(2,1)S(1)}, f32[16,1024]{1,0:T(8,128)S(1)}) custom-call(bf16[2048,256]{1,0:T(8,128)(2,1)S(1)} %get-tuple-element.24.query_part, f32[2048,128]{1,0:T(8,128)S(1)} %get-tuple-element.25.key_part, ...), custom_call_target="tpu_custom_call" | custom-call | tf_op jit(solution)/shard_map/give_back/pallas_call | solution.py:506
  160.4 1.0 copy.22
  161.3 0.7 copy.23
  162.0 0.7 copy.24
  162.7 0.6 copy.25
  (2 shorter events, 0.0 us)
Async XLA Ops:
  74.6 1.0 copy-start
  75.6 1.0 copy-start.1
  76.7 0.8 copy-start.2

commit v3 on v2

v3 whole, which is shorter than its diff:
```python
import functools

import jax
import jax.numpy as jnp
from jax import lax
from jax.experimental import pallas as pl
from jax.experimental.pallas import tpu as pltpu
from jax.sharding import PartitionSpec as P

HEADS = 32
KV_HEADS = 8
HEAD_DIM = 128
DOCS = 2
SCALE = HEAD_DIM ** (-0.5)
LOG2E = 1.4426950408889634
BLOCK = 512
ROWS = 128
UNITS = 16
NT = (((1,), (1,)), ((), ()))
TN = (((0,), (0,)), ((), ()))
NN = (((1,), (0,)), ((), ()))
MESH = pl.DeviceIdType.MESH
ANY = pl.BlockSpec(memory_space=pl.ANY)
VMEM = pl.BlockSpec(memory_space=pltpu.VMEM)
DMA = pltpu.SemaphoreType.DMA


def place():
    seq = lax.axis_index("seq")
    unit = lax.rem(seq, UNITS)
    return seq, seq - unit, unit, unit // 8, lax.rem(unit, 8)


def send(src, dst, send_sem, recv_sem, **device):
    copy = pltpu.make_async_remote_copy(
        src_ref=src,
        dst_ref=dst,
        send_sem=send_sem,
        recv_sem=recv_sem,
        device_id=device,
        device_id_type=MESH,
    )
    copy.start()


def drain(ref, sem):
    pltpu.make_async_copy(ref, ref, sem).wait()


def rows_of(block):
    return pl.ds(pl.multiple_of(block * ROWS, ROWS), ROWS)


def columns_of(block, width=HEAD_DIM):
    return pl.ds(pl.multiple_of(block * width, width), width)


def scores_of(key, query, total):
    scores = lax.dot_general(key, query, NT, preferred_element_type=jnp.float32)
    return jnp.exp2(scores * (SCALE * LOG2E) - total)


def kernel(
    query_ref,
    grad_ref,
    key_ref,
    value_ref,
    small_ref,
    hidden_ref,
    query_grad,
    key_grad,
    value_grad,
    weight_grad,
    query_unit,
    grad_unit,
    key_unit,
    value_unit,
    small_unit,
    hidden_unit,
    probs_kept,
    query_part,
    key_sum,
    value_sum,
    low,
    halves,
    staged,
    value_own,
    value_in,
    product,
    product_in,
    summed,
    piece,
    piece_in,
    final,
    final_in,
    own_sem,
    front_send,
    front_recv,
    pass_send,
    pass_recv,
    bulk_send,
    bulk_recv,
    hidden_send,
    hidden_recv,
    core_send,
    core_recv,
    half_send,
    half_recv,
    ring_send,
    ring_recv,
    query_send,
    query_recv,
    gather_send,
    gather_recv,
    cross_send,
    cross_recv,
    piece_send,
    piece_recv,
    final_send,
    final_recv,
):
    seq, base, unit, half, lane = place()
    dp = lax.axis_index("dp")
    across = seq // 8
    twin = dp + 1 - 2 * lax.rem(dp, 2)
    partner = base + (1 - half) * 8 + lane
    barrier = pltpu.get_barrier_semaphore()
    for step in range(1, UNITS):
        pl.semaphore_signal(
            barrier,
            inc=1,
            device_id={"seq": base + lax.rem(unit + step, UNITS)},
            device_id_type=MESH,
        )
    for step in range(1, 4):
        pl.semaphore_signal(
            barrier,
            inc=1,
            device_id={"seq": lax.rem(across + step, 4) * 8 + lane},
            device_id_type=MESH,
        )
    for step in range(1, 8):
        pl.semaphore_signal(
            barrier, inc=1, device_id={"dp": lax.rem(dp + step, 8)}, device_id_type=MESH
        )
    pl.semaphore_wait(barrier, 25)

    pairs = ((key_ref, key_unit), (value_ref, value_unit))
    for step in range(1, 8):
        target = lax.rem(lane + step, 8)
        for which, (source, landing) in enumerate(pairs):
            send(
                source.at[:, columns_of(target)],
                landing.at[rows_of(unit)],
                front_send.at[which],
                front_recv.at[which, lane],
                seq=base + half * 8 + target,
            )
    for which, (source, landing) in enumerate(pairs):
        send(
            source.at[:, columns_of(lane)],
            landing.at[rows_of(unit)],
            pass_send.at[which],
            pass_recv.at[which],
            seq=partner,
        )
    for head in range(2):
        for step in range(1, UNITS):
            target = lax.rem(unit + step, UNITS)
            columns = columns_of(lax.rem(target, 8) * 4 + (target // 8) * 2 + head)
            for which, (source, landing) in enumerate(
                ((query_ref, query_unit), (grad_ref, grad_unit))
            ):
                send(
                    source.at[:, columns],
                    landing.at[head, rows_of(unit)],
                    bulk_send.at[head * 2 + which],
                    bulk_recv.at[head * 2 + which],
                    seq=base + target,
                )
            if head == 0:
                send(
                    small_ref.at[target],
                    small_unit.at[unit],
                    bulk_send.at[4],
                    bulk_recv.at[4],
                    seq=base + target,
                )
        if head == 0:
            for step in (2, 1, 3):
                send(
                    hidden_ref,
                    hidden_unit.at[rows_of(dp)],
                    hidden_send,
                    hidden_recv.at[dp // 2],
                    dp=lax.rem(dp + 2 * step, 8),
                )
            send(hidden_ref, hidden_unit.at[rows_of(dp)], core_send, core_recv, dp=twin)
    mine = lane * 4 + half * 2
    own = (
        (key_ref.at[:, columns_of(lane)], key_unit.at[rows_of(unit)]),
        (value_ref.at[:, columns_of(lane)], value_unit.at[rows_of(unit)]),
        (small_ref.at[unit], small_unit.at[unit]),
        (query_ref.at[:, columns_of(mine)], query_unit.at[0, rows_of(unit)]),
        (grad_ref.at[:, columns_of(mine)], grad_unit.at[0, rows_of(unit)]),
        (query_ref.at[:, columns_of(mine + 1)], query_unit.at[1, rows_of(unit)]),
        (grad_ref.at[:, columns_of(mine + 1)], grad_unit.at[1, rows_of(unit)]),
        (hidden_ref, hidden_unit.at[rows_of(dp)]),
    )
    own = [pltpu.make_async_copy(*pair, own_sem.at[i]) for i, pair in enumerate(own)]
    for copy in own:
        copy.start()
    for step in range(1, 8):
        source = lax.rem(lane - step + 8, 8)
        for which, (_, landing) in enumerate(pairs):
            block = landing.at[rows_of(half * 8 + source)]
            drain(block, front_recv.at[which, source])
            send(block, block, pass_send.at[which], pass_recv.at[which], seq=partner)

    key_sum[...] = jnp.zeros_like(key_sum)
    value_sum[...] = jnp.zeros_like(value_sum)
    causal = lax.broadcasted_iota(jnp.int32, (BLOCK, BLOCK), 0) <= lax.broadcasted_iota(
        jnp.int32, (BLOCK, BLOCK), 1
    )
    per = BLOCK // ROWS
    positions = UNITS * ROWS // BLOCK

    def spread(position, row):
        return jnp.concatenate(
            [small_unit[position * per + t, row : row + 1, :] for t in range(per)], axis=1
        )

    def later(head, position, front, probs, query, grad, delta):
        fronts = pl.ds(front * BLOCK, BLOCK)
        key = key_unit[fronts, :]
        dprobs = lax.dot_general(
            value_unit[fronts, :], grad, NT, preferred_element_type=jnp.float32
        )
        dscores = (probs * (dprobs - delta)).astype(jnp.bfloat16)
        key_sum[fronts, :] += lax.dot_general(
            dscores, query, NN, preferred_element_type=jnp.float32
        )
        return lax.dot_general(dscores, key, TN, preferred_element_type=jnp.float32)

    def first(position, front, query, grad, total):
        fronts = pl.ds(front * BLOCK, BLOCK)
        probs = scores_of(key_unit[fronts, :], query, total)
        if front == position:
            probs = jnp.where(causal, probs, 0.0)
        value_sum[fronts, :] += lax.dot_general(
            probs.astype(jnp.bfloat16), grad, NN, preferred_element_type=jnp.float32
        )
        return probs

    def give_query(head):
        for step in range(1, UNITS):
            target = lax.rem(unit + step, UNITS)
            send(
                query_part.at[head, rows_of(target)],
                query_grad.at[:, columns_of(mine + head)],
                query_send.at[head],
                query_recv.at[head],
                seq=base + target,
            )
        pltpu.make_async_copy(
            query_part.at[head, rows_of(unit)],
            query_grad.at[:, columns_of(mine + head)],
            own_sem.at[8 + head],
        ).start()

    for copy in own[:5]:
        copy.wait()
    for which, (_, landing) in enumerate(pairs):
        drain(landing.at[pl.ds(0, 8 * ROWS)], pass_recv.at[which])
    some = pl.ds(0, 15 * ROWS)
    drain(query_unit.at[0, some], bulk_recv.at[0])
    drain(grad_unit.at[0, some], bulk_recv.at[1])
    drain(small_unit.at[pl.ds(0, 15)], bulk_recv.at[4])
    for position in range(positions):
        rows = pl.ds(position * BLOCK, BLOCK)
        query = query_unit[0, rows, :]
        grad = grad_unit[0, rows, :]
        total = spread(position, 0) * LOG2E
        delta = spread(position, 2)
        query_sum = None
        for front in range(position + 1):
            probs = first(position, front, query, grad, total)
            term = later(0, position, front, probs, query, grad, delta)
            query_sum = term if query_sum is None else query_sum + term
        query_part[0, rows, :] = (query_sum * SCALE).astype(jnp.bfloat16)
    give_query(0)

    for step in (1, 3, 2):
        source = lax.rem(dp + 2 * step, 8)
        arrived = hidden_unit.at[rows_of(source)]
        drain(arrived, hidden_recv.at[source // 2])
        send(arrived, arrived, core_send, core_recv, dp=twin)

    for copy in own[5:7]:
        copy.wait()
    drain(query_unit.at[1, some], bulk_recv.at[2])
    drain(grad_unit.at[1, some], bulk_recv.at[3])
    slot = 0
    for position in range(positions):
        rows = pl.ds(position * BLOCK, BLOCK)
        query = query_unit[1, rows, :]
        grad = grad_unit[1, rows, :]
        total = spread(position, 1) * LOG2E
        for front in range(position + 1):
            probs_kept[slot] = first(position, front, query, grad, total)
            slot += 1

    def give_half(which, array, factor):
        for step in range(8):
            target = lax.rem(lane + 1 + step, 8)
            low[which, target] = (array[rows_of((1 - half) * 8 + target), :] * factor).astype(
                jnp.bfloat16
            )
            send(
                low.at[which, target],
                halves.at[which, target],
                half_send.at[which],
                half_recv.at[which, target],
                seq=partner,
            )

    def give_whole(which, array, factor, landing):
        landing = landing.at[:, columns_of(lane)]
        for step in range(8):
            target = lax.rem(lane + 1 + step, 8)
            drain(halves.at[which, target], half_recv.at[which, target])
            staged[which, target] = (
                array[rows_of(half * 8 + target), :] * factor
                + halves[which, target].astype(jnp.float32)
            ).astype(jnp.bfloat16)
            if step < 7:
                send(
                    staged.at[which, target],
                    landing,
                    ring_send.at[which],
                    ring_recv.at[which],
                    seq=base + half * 8 + target,
                )
            else:
                pltpu.make_async_copy(
                    staged.at[which, target], landing, own_sem.at[10 + which]
                ).start()

    give_half(0, value_sum, 1.0)
    slot = 0
    for position in range(positions):
        rows = pl.ds(position * BLOCK, BLOCK)
        query = query_unit[1, rows, :]
        grad = grad_unit[1, rows, :]
        delta = spread(position, 3)
        query_sum = None
        for front in range(position + 1):
            term = later(1, position, front, probs_kept[slot], query, grad, delta)
            query_sum = term if query_sum is None else query_sum + term
            slot += 1
        query_part[1, rows, :] = (query_sum * SCALE).astype(jnp.bfloat16)
    give_half(1, key_sum, SCALE)
    give_whole(0, value_sum, 1.0, value_own)
    give_query(1)
    give_whole(1, key_sum, SCALE, key_grad)

    drain(staged.at[0, 0], own_sem.at[10])
    drain(staged.at[0, pl.ds(0, 7)], ring_recv.at[0])
    for step in range(1, 8):
        target = lax.rem(dp + step, 8)
        send(
            value_own.at[:, columns_of(target)],
            value_in.at[rows_of(dp)],
            gather_send,
            gather_recv,
            dp=target,
        )
    pltpu.make_async_copy(value_own, value_grad, own_sem.at[12]).start()
    value_in[rows_of(dp), :] = value_own[:, columns_of(dp)]
    own[7].wait()
    drain(hidden_unit.at[pl.ds(0, 4 * ROWS)], core_recv)
    drain(value_in.at[pl.ds(0, 7 * ROWS)], gather_recv)
    for step in range(4):
        target = lax.rem(across + 1 + step, 4)
        total = lax.dot_general(
            value_in[...],
            hidden_unit[:, columns_of(target, 8 * ROWS)],
            TN,
            preferred_element_type=jnp.float32,
        )
        if step < 3:
            product[target] = total.astype(jnp.bfloat16)
            send(
                product.at[target],
                product_in.at[across],
                cross_send,
                cross_recv,
                seq=target * 8 + lane,
            )
        else:
            summed[...] = total
    drain(product.at[pl.ds(0, 3)], cross_recv)
    for step in range(8):
        target = lax.rem(lane + 1 + step, 8)
        columns = columns_of(target)
        total = summed[:, columns]
        for source in range(1, 4):
            total = total + product_in[lax.rem(across + source, 4), :, columns].astype(jnp.float32)
        if step < 7:
            piece[target] = total
            send(
                piece.at[target],
                piece_in.at[lane],
                piece_send,
                piece_recv,
                seq=across * 8 + target,
            )
        else:
            piece_in[lane] = total
    drain(piece.at[pl.ds(0, 7)], piece_recv)
    total = piece_in[0]
    for step in range(1, 8):
        total = total + piece_in[step]
    final[...] = total.T
    for step in range(1, 8):
        target = lax.rem(dp + step, 8)
        send(
            final.at[pl.ds(pl.multiple_of(target * 16, 16), 16)],
            final_in.at[:, columns_of(dp)],
            final_send,
            final_recv,
            dp=target,
        )
    final_in[:, columns_of(dp)] = final[pl.ds(pl.multiple_of(dp * 16, 16), 16), :]
    drain(final.at[pl.ds(0, 7 * 16)], final_recv)
    weight_grad[...] = final_in[...]

    for which, (_, landing) in enumerate(pairs):
        drain(landing.at[pl.ds(0, 7 * ROWS)], front_send.at[which])
        drain(landing.at[pl.ds(0, 8 * ROWS)], pass_send.at[which])
    for which in range(4):
        drain(query_unit.at[0, some], bulk_send.at[which])
    drain(small_unit.at[pl.ds(0, 15)], bulk_send.at[4])
    drain(hidden_unit.at[pl.ds(0, 3 * ROWS)], hidden_send)
    drain(hidden_unit.at[pl.ds(0, 4 * ROWS)], core_send)
    drain(staged.at[1, 0], own_sem.at[11])
    drain(value_own, own_sem.at[12])
    drain(staged.at[1, pl.ds(0, 7)], ring_recv.at[1])
    for head in range(2):
        drain(query_part.at[head, rows_of(0)], own_sem.at[8 + head])
        drain(query_part.at[head, some], query_recv.at[head])
        drain(query_part.at[head, some], query_send.at[head])
    for which in range(2):
        drain(halves.at[which], half_send.at[which])
        drain(staged.at[which, pl.ds(0, 7)], ring_send.at[which])
    drain(value_in.at[pl.ds(0, 7 * ROWS)], gather_send)
    drain(product.at[pl.ds(0, 3)], cross_send)
    drain(piece.at[pl.ds(0, 7)], piece_send)
    drain(final.at[pl.ds(0, 7 * 16)], final_send)


def backward(queries, out_grad, keys, values, small, hidden):
    low = jnp.bfloat16
    wide = jnp.float32
    columns = KV_HEADS * HEAD_DIM
    length = UNITS * ROWS
    positions = length // BLOCK
    slots = positions * (positions + 1) // 2
    return pl.pallas_call(
        kernel,
        out_shape=(
            jax.ShapeDtypeStruct((ROWS, HEADS * HEAD_DIM), low),
            jax.ShapeDtypeStruct((ROWS, columns), low),
            jax.ShapeDtypeStruct((ROWS, columns), low),
            jax.ShapeDtypeStruct((16, columns), wide),
        ),
        in_specs=[ANY] * 6,
        out_specs=(ANY, ANY, ANY, VMEM),
        scratch_shapes=[
            pltpu.VMEM((2, length, HEAD_DIM), low),
            pltpu.VMEM((2, length, HEAD_DIM), low),
            pltpu.VMEM((length, HEAD_DIM), low),
            pltpu.VMEM((length, HEAD_DIM), low),
            pltpu.VMEM((UNITS, 8, ROWS), wide),
            pltpu.VMEM((8 * ROWS, HEADS * HEAD_DIM), low),
            pltpu.VMEM((slots, BLOCK, BLOCK), wide),
            pltpu.VMEM((2, length, HEAD_DIM), low),
            pltpu.VMEM((length, HEAD_DIM), wide),
            pltpu.VMEM((length, HEAD_DIM), wide),
            pltpu.VMEM((2, 8, ROWS, HEAD_DIM), low),
            pltpu.VMEM((2, 8, ROWS, HEAD_DIM), low),
            pltpu.VMEM((2, 8, ROWS, HEAD_DIM), low),
            pltpu.VMEM((ROWS, columns), low),
            pltpu.VMEM((8 * ROWS, HEAD_DIM), low),
            pltpu.VMEM((4, ROWS, columns), low),
            pltpu.VMEM((4, ROWS, columns), low),
            pltpu.VMEM((ROWS, columns), wide),
            pltpu.VMEM((8, ROWS, ROWS), wide),
            pltpu.VMEM((8, ROWS, ROWS), wide),
            pltpu.VMEM((ROWS, ROWS), wide),
            pltpu.VMEM((16, columns), wide),
            DMA((13,)),
            DMA((2,)),
            DMA((2, 8)),
            DMA((2,)),
            DMA((2,)),
            DMA((5,)),
            DMA((5,)),
            DMA,
            DMA((4,)),
            DMA,
            DMA,
            DMA((2,)),
            DMA((2, 8)),
            DMA((2,)),
            DMA((2,)),
            DMA((2,)),
            DMA((2,)),
        ]
        + [DMA] * 8,
        compiler_params=pltpu.CompilerParams(
            collective_id=0, has_side_effects=True, vmem_limit_bytes=56 * 1024 * 1024
        ),
        name="backward",
    )(queries, out_grad, keys, values, small, hidden)


def body(hidden_in, queries, keys, values, attn_out, out_grad, log_totals):
    delta = jnp.sum(
        (out_grad[0].astype(jnp.float32) * attn_out[0].astype(jnp.float32)).reshape(
            ROWS, HEADS, HEAD_DIM
        ),
        axis=2,
    )

    def by_unit(array):
        return array.reshape(ROWS, 8, 2, 2).transpose(2, 1, 3, 0).reshape(UNITS, 2, ROWS)

    small = jnp.concatenate(
        [by_unit(log_totals[0]), by_unit(delta), jnp.zeros((UNITS, 4, ROWS), jnp.float32)], axis=1
    )
    query_grad, key_grad, value_grad, weight_grad = backward(
        queries[0], out_grad[0], keys[0], values[0], small, hidden_in[0]
    )
    return (query_grad[None], key_grad[None], value_grad[None], weight_grad)


def solution(mesh):
    rows = P("dp", "seq", None)
    return jax.shard_map(
        body,
        mesh=mesh,
        in_specs=(rows,) * 7,
        out_specs=(rows, rows, rows, P(("seq", "dp"), None)),
        check_vma=False,
    )
```

time: 164 us -> 139 us (0.85)
  Pallas kernels: 152 us -> 130 us
  local copies, waits for them, and re-layouts: 7.17 us -> 4.93 us
    pallas_call x3 -> x1, Pallas kernels: 152 us -> 130 us  [backward(): pl.pallas_call(kernel, out_shape=(jax.ShapeDtypeStruct((ROWS, HEADS * HEA...]
    unnamed x11 -> x13, local copies, waits for them, and re-layouts: 6.29 us -> 4.77 us
where the time goes in v3:
time: 139 us; the launch traced here: 138 us
  Pallas kernels  130 us (94%)
  local copies, waits for them, and re-layouts  4.93 us (4%)
  other arithmetic  3.11 us (2%)
    pallas_call x1, Pallas kernels, backward(): pl.pallas_call(kernel, out_shape=(jax.ShapeDtypeStruct((ROWS, HEADS * HEA...  130 us
    unnamed x13, local copies, waits for them, and re-layouts  4.77 us

profile of v3, /device:TPU:1, one launch (start us, length us, event | category | flops | bytes accessed | tf_op | source)
XLA Modules:
  0.0 138.5 jit_solution(5138859240501014538)
XLA Ops:
  0.6 1.8 %multiply_bitcast_fusion = f32[16,8,32,128]{3,1,2,0:T(8,128)S(1)} fusion(bf16[1,128,4096]{2,1,0:T(8,128)(2,1)} %param.11, bf16[1,128,4096]{2,1,0:T(8,128)(2,1)} %param.12), kind=kLoop, calls=%fused_computation | loop fusion | flops 1572864 | bytes 4194304
  2.4 0.4 copy.17
  2.8 0.0 copy-start.3
  2.8 0.6 reduce_sum.9
  3.4 0.1 copy.15
  3.5 0.0 copy-done.3
  3.6 0.1 pad.2.clone
  3.6 0.7 maximum_maximum_fusion.small_ref
  4.3 129.7 %backward.1 = (bf16[128,4096]{1,0:T(8,128)(2,1)}, bf16[128,1024]{1,0:T(8,128)(2,1)}, bf16[128,1024]{1,0:T(8,128)(2,1)}, f32[16,1024]{1,0:T(8,128)}) custom-call(bf16[128,4096]{1,0:T(8,128)(2,1)} %bitcast.22, bf16[128,4096]{1,0:T(8,128)(2,1)} %bitcast.21, bf16[128,1024]{1,0:T(8,128)(2,1)} %bitcast.25, bf16[128,1024]{1,0:T(8,128)(2,1)} %bitcast.26, ...), custom_call_target="tpu_custom_call" | custom-call | tf_op jit(solution)/shard_map/backward/pallas_call | solution.py:469
  134.1 0.0 copy-start.1
  134.1 0.0 copy-start
  134.1 0.0 copy-start.2
  134.1 2.3 %copy.22 = bf16[1,128,4096]{2,1,0:T(8,128)(2,1)} copy(bf16[1,128,4096]{2,1,0:T(8,128)(2,1)} %bitcast.24) | data formatting | bytes 2097152
  136.4 0.0 copy-done.1
  136.4 0.7 copy.23
  137.1 0.0 copy-done
  137.1 0.7 copy.24
  137.8 0.0 copy-done.2
  137.8 0.6 copy.25
  (3 shorter events, 0.0 us)
Async XLA Ops:
  2.8 0.7 copy-start.3
  134.1 2.4 %copy-start.1 = (bf16[128,1024]{1,0:T(8,128)(2,1)S(1)}, bf16[128,1024]{1,0:T(8,128)(2,1)}, u32[]{:S(2)}) copy-start(bf16[128,1024]{1,0:T(8,128)(2,1)} %get-tuple-element.9) | copy-start | bytes 786436
  134.1 3.1 %copy-start = (bf16[128,1024]{1,0:T(8,128)(2,1)S(1)}, bf16[128,1024]{1,0:T(8,128)(2,1)}, u32[]{:S(2)}) copy-start(bf16[128,1024]{1,0:T(8,128)(2,1)} %get-tuple-element.10) | copy-start | bytes 786436
  134.1 3.8 %copy-start.2 = (f32[16,1024]{1,0:T(8,128)S(1)}, f32[16,1024]{1,0:T(8,128)}, u32[]{:S(2)}) copy-start(f32[16,1024]{1,0:T(8,128)} %get-tuple-element.19) | copy-start | bytes 196612

commit v4 on v3

--- a/solution.py
+++ b/solution.py
@@ -10,7 +10,6 @@
 HEADS = 32
 KV_HEADS = 8
 HEAD_DIM = 128
-DOCS = 2
 SCALE = HEAD_DIM ** (-0.5)
 LOG2E = 1.4426950408889634
 BLOCK = 512
@@ -19,6 +18,8 @@
 NT = (((1,), (1,)), ((), ()))
 TN = (((0,), (0,)), ((), ()))
 NN = (((1,), (0,)), ((), ()))
+RING = (4, 1, 7, 2, 6, 3, 5)
+TURNS = tuple((flip, step) for step in (4, 1, 7, 2, 6, 3, 5, 0) for flip in (0, 1))[:-2] + ((1, 0),)
 MESH = pl.DeviceIdType.MESH
 ANY = pl.BlockSpec(memory_space=pl.ANY)
 VMEM = pl.BlockSpec(memory_space=pltpu.VMEM)
@@ -65,7 +66,8 @@
     grad_ref,
     key_ref,
     value_ref,
-    small_ref,
+    output_ref,
+    total_ref,
     hidden_ref,
     query_grad,
     key_grad,
@@ -77,6 +79,10 @@
     value_unit,
     small_unit,
     hidden_unit,
+    grad_own,
+    output_own,
+    total_own,
+    small_own,
     probs_kept,
     query_part,
     key_sum,
@@ -86,8 +92,6 @@
     staged,
     value_own,
     value_in,
-    product,
-    product_in,
     summed,
     piece,
     piece_in,
@@ -112,8 +116,8 @@
     query_recv,
     gather_send,
     gather_recv,
-    cross_send,
-    cross_recv,
+    side_send,
+    side_recv,
     piece_send,
     piece_recv,
     final_send,
@@ -124,6 +128,10 @@
     across = seq // 8
     twin = dp + 1 - 2 * lax.rem(dp, 2)
     partner = base + (1 - half) * 8 + lane
+
+    def turned(flip, step):
+        return (half + flip - 2 * half * flip) * 8 + lax.rem(lane + step, 8)
+
     barrier = pltpu.get_barrier_semaphore()
     for step in range(1, UNITS):
         pl.semaphore_signal(
@@ -132,21 +140,29 @@
             device_id={"seq": base + lax.rem(unit + step, UNITS)},
             device_id_type=MESH,
         )
-    for step in range(1, 4):
-        pl.semaphore_signal(
-            barrier,
-            inc=1,
-            device_id={"seq": lax.rem(across + step, 4) * 8 + lane},
-            device_id_type=MESH,
-        )
-    for step in range(1, 8):
-        pl.semaphore_signal(
-            barrier, inc=1, device_id={"dp": lax.rem(dp + step, 8)}, device_id_type=MESH
-        )
-    pl.semaphore_wait(barrier, 25)
+    for over in (2, 1, 3, 0):
+        for step in range(8):
+            if over or step:
+                pl.semaphore_signal(
+                    barrier,
+                    inc=1,
+                    device_id={
+                        "seq": lax.rem(across + over, 4) * 8 + lane,
+                        "dp": lax.rem(dp + step, 8),
+                    },
+                    device_id_type=MESH,
+                )
+    rows_own = (
+        pltpu.make_async_copy(grad_ref, grad_own, own_sem.at[13]),
+        pltpu.make_async_copy(output_ref, output_own, own_sem.at[14]),
+        pltpu.make_async_copy(total_ref, total_own, own_sem.at[15]),
+    )
+    for copy in rows_own:
+        copy.start()
+    pl.semaphore_wait(barrier, 46)
 
     pairs = ((key_ref, key_unit), (value_ref, value_unit))
-    for step in range(1, 8):
+    for step in RING:
         target = lax.rem(lane + step, 8)
         for which, (source, landing) in enumerate(pairs):
             send(
@@ -164,9 +180,32 @@
             pass_recv.at[which],
             seq=partner,
         )
+    for over in (2, 1, 3):
+        target = lax.rem(across + over, 4)
+        send(
+            hidden_ref.at[:, columns_of(target, 8 * ROWS)],
+            hidden_unit.at[rows_of(across * 8 + dp)],
+            side_send,
+            side_recv.at[across],
+            seq=target * 8 + lane,
+        )
+
+    def along(block, source, row):
+        for step in (2, 1, 3):
+            send(
+                block,
+                hidden_unit.at[row],
+                hidden_send,
+                hidden_recv.at[source, dp // 2],
+                dp=lax.rem(dp + 2 * step, 8),
+            )
+        send(block, hidden_unit.at[row], core_send, core_recv, dp=twin)
+
+    quarter = hidden_ref.at[:, columns_of(across, 8 * ROWS)]
+    along(quarter, across, rows_of(across * 8 + dp))
     for head in range(2):
-        for step in range(1, UNITS):
-            target = lax.rem(unit + step, UNITS)
+        for flip, step in TURNS:
+            target = turned(flip, step)
             columns = columns_of(lax.rem(target, 8) * 4 + (target // 8) * 2 + head)
             for which, (source, landing) in enumerate(
                 ((query_ref, query_unit), (grad_ref, grad_unit))
@@ -178,44 +217,59 @@
                     bulk_recv.at[head * 2 + which],
                     seq=base + target,
                 )
-            if head == 0:
-                send(
-                    small_ref.at[target],
-                    small_unit.at[unit],
-                    bulk_send.at[4],
-                    bulk_recv.at[4],
-                    seq=base + target,
-                )
-        if head == 0:
-            for step in (2, 1, 3):
-                send(
-                    hidden_ref,
-                    hidden_unit.at[rows_of(dp)],
-                    hidden_send,
-                    hidden_recv.at[dp // 2],
-                    dp=lax.rem(dp + 2 * step, 8),
-                )
-            send(hidden_ref, hidden_unit.at[rows_of(dp)], core_send, core_recv, dp=twin)
+    for copy in rows_own:
+        copy.wait()
+    column = lax.broadcasted_iota(jnp.int32, (ROWS, ROWS), 1)
+    delta = jnp.zeros((ROWS, ROWS), jnp.float32)
+    for head in range(HEADS):
+        columns = slice(head * HEAD_DIM, (head + 1) * HEAD_DIM)
+        row = jnp.sum(
+            grad_own[:, columns].astype(jnp.float32) * output_own[:, columns].astype(jnp.float32),
+            axis=1,
+            keepdims=True,
+        )
+        delta = jnp.where(column == head, row, delta)
+    delta = delta.T
+    totals = total_own[...]
+    for target in range(UNITS):
+        head = (target % 8) * 4 + (target // 8) * 2
+        small_own[target, 0:2, :] = totals[head : head + 2, :]
+        small_own[target, 2:4, :] = delta[head : head + 2, :]
+    for flip, step in TURNS:
+        target = turned(flip, step)
+        send(
+            small_own.at[target],
+            small_unit.at[unit],
+            bulk_send.at[4],
+            bulk_recv.at[4],
+            seq=base + target,
+        )
+    small_unit[unit] = small_own[unit]
     mine = lane * 4 + half * 2
     own = (
         (key_ref.at[:, columns_of(lane)], key_unit.at[rows_of(unit)]),
         (value_ref.at[:, columns_of(lane)], value_unit.at[rows_of(unit)]),
-        (small_ref.at[unit], small_unit.at[unit]),
         (query_ref.at[:, columns_of(mine)], query_unit.at[0, rows_of(unit)]),
         (grad_ref.at[:, columns_of(mine)], grad_unit.at[0, rows_of(unit)]),
         (query_ref.at[:, columns_of(mine + 1)], query_unit.at[1, rows_of(unit)]),
         (grad_ref.at[:, columns_of(mine + 1)], grad_unit.at[1, rows_of(unit)]),
-        (hidden_ref, hidden_unit.at[rows_of(dp)]),
+        (quarter, hidden_unit.at[rows_of(across * 8 + dp)]),
     )
     own = [pltpu.make_async_copy(*pair, own_sem.at[i]) for i, pair in enumerate(own)]
     for copy in own:
         copy.start()
-    for step in range(1, 8):
+    for step in RING:
         source = lax.rem(lane - step + 8, 8)
         for which, (_, landing) in enumerate(pairs):
             block = landing.at[rows_of(half * 8 + source)]
             drain(block, front_recv.at[which, source])
             send(block, block, pass_send.at[which], pass_recv.at[which], seq=partner)
+
+    for over in (1, 3, 2):
+        source = lax.rem(across + over, 4)
+        row = rows_of(source * 8 + dp)
+        drain(hidden_unit.at[row], side_recv.at[source])
+        along(hidden_unit.at[row], source, row)
 
     key_sum[...] = jnp.zeros_like(key_sum)
     value_sum[...] = jnp.zeros_like(value_sum)
@@ -253,8 +307,8 @@
         return probs
 
     def give_query(head):
-        for step in range(1, UNITS):
-            target = lax.rem(unit + step, UNITS)
+        for flip, step in TURNS:
+            target = turned(flip, step)
             send(
                 query_part.at[head, rows_of(target)],
                 query_grad.at[:, columns_of(mine + head)],
@@ -268,7 +322,7 @@
             own_sem.at[8 + head],
         ).start()
 
-    for copy in own[:5]:
+    for copy in own[:4]:
         copy.wait()
     for which, (_, landing) in enumerate(pairs):
         drain(landing.at[pl.ds(0, 8 * ROWS)], pass_recv.at[which])
@@ -288,18 +342,12 @@
             term = later(0, position, front, probs, query, grad, delta)
             query_sum = term if query_sum is None else query_sum + term
         query_part[0, rows, :] = (query_sum * SCALE).astype(jnp.bfloat16)
-    give_query(0)
-
-    for step in (1, 3, 2):
-        source = lax.rem(dp + 2 * step, 8)
-        arrived = hidden_unit.at[rows_of(source)]
-        drain(arrived, hidden_recv.at[source // 2])
-        send(arrived, arrived, core_send, core_recv, dp=twin)
-
-    for copy in own[5:7]:
+
+    for copy in own[4:6]:
         copy.wait()
     drain(query_unit.at[1, some], bulk_recv.at[2])
     drain(grad_unit.at[1, some], bulk_recv.at[3])
+    give_query(0)
     slot = 0
     for position in range(positions):
         rows = pl.ds(position * BLOCK, BLOCK)
@@ -311,8 +359,8 @@
             slot += 1
 
     def give_half(which, array, factor):
-        for step in range(8):
-            target = lax.rem(lane + 1 + step, 8)
+        for step in RING + (0,):
+            target = lax.rem(lane + step, 8)
             low[which, target] = (array[rows_of((1 - half) * 8 + target), :] * factor).astype(
                 jnp.bfloat16
             )
@@ -326,19 +374,19 @@
 
     def give_whole(which, array, factor, landing):
         landing = landing.at[:, columns_of(lane)]
-        for step in range(8):
-            target = lax.rem(lane + 1 + step, 8)
+        for step in RING + (0,):
+            target = lax.rem(lane + step, 8)
             drain(halves.at[which, target], half_recv.at[which, target])
             staged[which, target] = (
                 array[rows_of(half * 8 + target), :] * factor
                 + halves[which, target].astype(jnp.float32)
             ).astype(jnp.bfloat16)
-            if step < 7:
+            if step:
                 send(
                     staged.at[which, target],
                     landing,
                     ring_send.at[which],
-                    ring_recv.at[which],
+                    ring_recv.at[which, lane],
                     seq=base + half * 8 + target,
                 )
             else:
@@ -362,65 +410,60 @@
     give_half(1, key_sum, SCALE)
     give_whole(0, value_sum, 1.0, value_own)
     give_query(1)
+    for over in range(4):
+        for step in (1, 3, 2):
+            source = lax.rem(dp + 2 * step, 8)
+            arrived = hidden_unit.at[rows_of(over * 8 + source)]
+            drain(arrived, hidden_recv.at[over, source // 2])
+            send(arrived, arrived, core_send, core_recv, dp=twin)
+
+    for step in (0,) + RING:
+        group = lax.rem(lane - step + 8, 8)
+        block = value_own.at[:, columns_of(group)]
+        if step:
+            drain(staged.at[0, 0], ring_recv.at[0, group])
+        else:
+            drain(staged.at[0, 0], own_sem.at[10])
+
+        def give_block(over):
+            send(
+                block,
+                value_in.at[rows_of(across * 8 + dp)],
+                gather_send,
+                gather_recv.at[across],
+                seq=lax.rem(across + over, 4) * 8 + lane,
+                dp=group,
+            )
+
+        for over in (2, 1, 3):
+            give_block(over)
+        pl.when(group != dp)(functools.partial(give_block, 0))
+
+    pltpu.make_async_copy(value_own, value_grad, own_sem.at[12]).start()
+    value_in[rows_of(across * 8 + dp), :] = value_own[:, columns_of(dp)]
     give_whole(1, key_sum, SCALE, key_grad)
-
-    drain(staged.at[0, 0], own_sem.at[10])
-    drain(staged.at[0, pl.ds(0, 7)], ring_recv.at[0])
+    own[6].wait()
+    drain(hidden_unit.at[pl.ds(0, 16 * ROWS)], core_recv)
+    for over in (0, 1, 3, 2):
+        source = lax.rem(across + over, 4)
+        drain(value_in.at[pl.ds(0, (8 if over else 7) * ROWS)], gather_recv.at[source])
+        rows = pl.ds(pl.multiple_of(source * 8 * ROWS, 8 * ROWS), 8 * ROWS)
+        total = lax.dot_general(
+            value_in[rows, :], hidden_unit[rows, :], TN, preferred_element_type=jnp.float32
+        )
+        if over == 0:
+            summed[...] = total
+        else:
+            summed[...] += total
+    for step in RING:
+        target = lax.rem(lane + step, 8)
+        piece[target] = summed[:, columns_of(target)].astype(jnp.bfloat16)
+        send(piece.at[target], piece_in.at[lane], piece_send, piece_recv, seq=across * 8 + target)
+    final[...] = summed[:, columns_of(lane)]
+    drain(piece.at[pl.ds(0, 7)], piece_recv)
+    total = final[...]
     for step in range(1, 8):
-        target = lax.rem(dp + step, 8)
-        send(
-            value_own.at[:, columns_of(target)],
-            value_in.at[rows_of(dp)],
-            gather_send,
-            gather_recv,
-            dp=target,
-        )
-    pltpu.make_async_copy(value_own, value_grad, own_sem.at[12]).start()
-    value_in[rows_of(dp), :] = value_own[:, columns_of(dp)]
-    own[7].wait()
-    drain(hidden_unit.at[pl.ds(0, 4 * ROWS)], core_recv)
-    drain(value_in.at[pl.ds(0, 7 * ROWS)], gather_recv)
-    for step in range(4):
-        target = lax.rem(across + 1 + step, 4)
-        total = lax.dot_general(
-            value_in[...],
-            hidden_unit[:, columns_of(target, 8 * ROWS)],
-            TN,
-            preferred_element_type=jnp.float32,
-        )
-        if step < 3:
-            product[target] = total.astype(jnp.bfloat16)
-            send(
-                product.at[target],
-                product_in.at[across],
-                cross_send,
-                cross_recv,
-                seq=target * 8 + lane,
-            )
-        else:
-            summed[...] = total
-    drain(product.at[pl.ds(0, 3)], cross_recv)
-    for step in range(8):
-        target = lax.rem(lane + 1 + step, 8)
-        columns = columns_of(target)
-        total = summed[:, columns]
-        for source in range(1, 4):
-            total = total + product_in[lax.rem(across + source, 4), :, columns].astype(jnp.float32)
-        if step < 7:
-            piece[target] = total
-            send(
-                piece.at[target],
-                piece_in.at[lane],
-                piece_send,
-                piece_recv,
-                seq=across * 8 + target,
-            )
-        else:
-            piece_in[lane] = total
-    drain(piece.at[pl.ds(0, 7)], piece_recv)
-    total = piece_in[0]
-    for step in range(1, 8):
-        total = total + piece_in[step]
+        total = total + piece_in[lax.rem(lane + step, 8)].astype(jnp.float32)
     final[...] = total.T
     for step in range(1, 8):
         target = lax.rem(dp + step, 8)
@@ -441,11 +484,13 @@
     for which in range(4):
         drain(query_unit.at[0, some], bulk_send.at[which])
     drain(small_unit.at[pl.ds(0, 15)], bulk_send.at[4])
-    drain(hidden_unit.at[pl.ds(0, 3 * ROWS)], hidden_send)
-    drain(hidden_unit.at[pl.ds(0, 4 * ROWS)], core_send)
+    drain(hidden_unit.at[pl.ds(0, 3 * ROWS)], side_send)
+    drain(hidden_unit.at[pl.ds(0, 12 * ROWS)], hidden_send)
+    drain(hidden_unit.at[pl.ds(0, 16 * ROWS)], core_send)
     drain(staged.at[1, 0], own_sem.at[11])
     drain(value_own, own_sem.at[12])
-    drain(staged.at[1, pl.ds(0, 7)], ring_recv.at[1])
+    for step in RING:
+        drain(staged.at[1, 0], ring_recv.at[1, lax.rem(lane - step + 8, 8)])
     for head in range(2):
         drain(query_part.at[head, rows_of(0)], own_sem.at[8 + head])
         drain(query_part.at[head, some], query_recv.at[head])
@@ -453,13 +498,12 @@
     for which in range(2):
         drain(halves.at[which], half_send.at[which])
         drain(staged.at[which, pl.ds(0, 7)], ring_send.at[which])
-    drain(value_in.at[pl.ds(0, 7 * ROWS)], gather_send)
-    drain(product.at[pl.ds(0, 3)], cross_send)
+    drain(value_in.at[pl.ds(0, 31 * ROWS)], gather_send)
     drain(piece.at[pl.ds(0, 7)], piece_send)
     drain(final.at[pl.ds(0, 7 * 16)], final_send)
 
 
-def backward(queries, out_grad, keys, values, small, hidden):
+def backward(queries, out_grad, keys, values, attn_out, log_totals, hidden):
     low = jnp.bfloat16
     wide = jnp.float32
     columns = KV_HEADS * HEAD_DIM
@@ -474,15 +518,19 @@
             jax.ShapeDtypeStruct((ROWS, columns), low),
             jax.ShapeDtypeStruct((16, columns), wide),
         ),
-        in_specs=[ANY] * 6,
+        in_specs=[ANY] * 7,
         out_specs=(ANY, ANY, ANY, VMEM),
         scratch_shapes=[
             pltpu.VMEM((2, length, HEAD_DIM), low),
             pltpu.VMEM((2, length, HEAD_DIM), low),
             pltpu.VMEM((length, HEAD_DIM), low),
             pltpu.VMEM((length, HEAD_DIM), low),
-            pltpu.VMEM((UNITS, 8, ROWS), wide),
-            pltpu.VMEM((8 * ROWS, HEADS * HEAD_DIM), low),
+            pltpu.VMEM((UNITS, 4, ROWS), wide),
+            pltpu.VMEM((4 * 8 * ROWS, 8 * ROWS), low),
+            pltpu.VMEM((ROWS, HEADS * HEAD_DIM), low),
+            pltpu.VMEM((ROWS, HEADS * HEAD_DIM), low),
+            pltpu.VMEM((HEADS, ROWS), wide),
+            pltpu.VMEM((UNITS, 4, ROWS), wide),
             pltpu.VMEM((slots, BLOCK, BLOCK), wide),
             pltpu.VMEM((2, length, HEAD_DIM), low),
             pltpu.VMEM((length, HEAD_DIM), wide),
@@ -491,15 +539,13 @@
             pltpu.VMEM((2, 8, ROWS, HEAD_DIM), low),
             pltpu.VMEM((2, 8, ROWS, HEAD_DIM), low),
             pltpu.VMEM((ROWS, columns), low),
-            pltpu.VMEM((8 * ROWS, HEAD_DIM), low),
-            pltpu.VMEM((4, ROWS, columns), low),
-            pltpu.VMEM((4, ROWS, columns), low),
-            pltpu.VMEM((ROWS, columns), wide),
-            pltpu.VMEM((8, ROWS, ROWS), wide),
-            pltpu.VMEM((8, ROWS, ROWS), wide),
+            pltpu.VMEM((4 * 8 * ROWS, HEAD_DIM), low),
+            pltpu.VMEM((ROWS, 8 * ROWS), wide),
+            pltpu.VMEM((8, ROWS, ROWS), low),
+            pltpu.VMEM((8, ROWS, ROWS), low),
             pltpu.VMEM((ROWS, ROWS), wide),
             pltpu.VMEM((16, columns), wide),
-            DMA((13,)),
+            DMA((16,)),
             DMA((2,)),
             DMA((2, 8)),
             DMA((2,)),
@@ -507,40 +553,68 @@
             DMA((5,)),
             DMA((5,)),
             DMA,
-            DMA((4,)),
+            DMA((4, 4)),
             DMA,
             DMA,
             DMA((2,)),
             DMA((2, 8)),
             DMA((2,)),
-            DMA((2,)),
+            DMA((2, 8)),
             DMA((2,)),
             DMA((2,)),
         ]
-        + [DMA] * 8,
+        + [DMA, DMA((4,)), DMA, DMA((4,)), DMA, DMA, DMA, DMA],
         compiler_params=pltpu.CompilerParams(
             collective_id=0, has_side_effects=True, vmem_limit_bytes=56 * 1024 * 1024
         ),
         name="backward",
-    )(queries, out_grad, keys, values, small, hidden)
+    )(queries, out_grad, keys, values, attn_out, log_totals, hidden)
+
+
+def settle_kernel(*refs):
+    sources, results, held, come, go = refs[:4], refs[4:8], refs[8:12], refs[12], refs[13]
+    pieces = [(0, pl.ds(32 * i, 32)) for i in range(4)]
+    pieces += [(i, pl.ds(0, sources[i].shape[0])) for i in range(1, 4)]
+    loads = [
+        pltpu.make_async_copy(sources[i].at[rows], held[i].at[rows], come.at[n])
+        for n, (i, rows) in enumerate(pieces)
+    ]
+    stores = [
+        pltpu.make_async_copy(held[i].at[rows], results[i].at[rows], go.at[n])
+        for n, (i, rows) in enumerate(pieces)
+    ]
+    for load in loads:
+        load.start()
+    for load, store in zip(loads, stores):
+        load.wait()
+        store.start()
+    for store in stores:
+        store.wait()
+
+
+def settle(*arrays):
+    return pl.pallas_call(
+        settle_kernel,
+        out_shape=tuple(jax.ShapeDtypeStruct(array.shape, array.dtype) for array in arrays),
+        in_specs=[ANY] * 4,
+        out_specs=(ANY,) * 4,
+        scratch_shapes=[pltpu.VMEM(array.shape, array.dtype) for array in arrays]
+        + [DMA((7,)), DMA((7,))],
+        name="settle",
+    )(*arrays)
 
 
 def body(hidden_in, queries, keys, values, attn_out, out_grad, log_totals):
-    delta = jnp.sum(
-        (out_grad[0].astype(jnp.float32) * attn_out[0].astype(jnp.float32)).reshape(
-            ROWS, HEADS, HEAD_DIM
-        ),
-        axis=2,
-    )
-
-    def by_unit(array):
-        return array.reshape(ROWS, 8, 2, 2).transpose(2, 1, 3, 0).reshape(UNITS, 2, ROWS)
-
-    small = jnp.concatenate(
-        [by_unit(log_totals[0]), by_unit(delta), jnp.zeros((UNITS, 4, ROWS), jnp.float32)], axis=1
-    )
-    query_grad, key_grad, value_grad, weight_grad = backward(
-        queries[0], out_grad[0], keys[0], values[0], small, hidden_in[0]
+    query_grad, key_grad, value_grad, weight_grad = settle(
+        *backward(
+            queries[0],
+            out_grad[0],
+            keys[0],
+            values[0],
+            attn_out[0],
+            log_totals[0].T,
+            hidden_in[0],
+        )
     )
     return (query_grad[None], key_grad[None], value_grad[None], weight_grad)
 

time: 139 us -> 133 us (0.957)
  local copies, waits for them, and re-layouts: 4.93 us -> 0 us
  other arithmetic: 3.11 us -> 0 us
  Pallas kernels: 130 us -> 132 us
    unnamed x13 -> x0, local copies, waits for them, and re-layouts: 4.77 us -> none
    pallas_call x0 -> x1, Pallas kernels: none -> 2.22 us  [settle(): pl.pallas_call(settle_kernel, out_shape=tuple((jax.ShapeDtypeStruct(array...]
    unnamed x1 -> x0, other arithmetic: 1.8 us -> none
where the time goes in v4:
time: 133 us
  Pallas kernels  132 us (99%)
    pallas_call x1, Pallas kernels, backward(): pl.pallas_call(kernel, out_shape=(jax.ShapeDtypeStruct((ROWS, HEADS * HEA...  130 us

profile of v4, /device:TPU:1, one launch (start us, length us, event | category | flops | bytes accessed | tf_op | source)
XLA Modules:
  0.0 133.2 jit_solution(16796559618713887334)
XLA Ops:
  0.6 130.2 %backward.1 = (bf16[128,4096]{1,0:T(8,128)(2,1)}, bf16[128,1024]{1,0:T(8,128)(2,1)}, bf16[128,1024]{1,0:T(8,128)(2,1)}, f32[16,1024]{1,0:T(8,128)}) custom-call(bf16[128,4096]{1,0:T(8,128)(2,1)} %bitcast.12, bf16[128,4096]{1,0:T(8,128)(2,1)} %bitcast.13, bf16[128,1024]{1,0:T(8,128)(2,1)} %bitcast.16, bf16[128,1024]{1,0:T(8,128)(2,1)} %bitcast.17, ...), custom_call_target="tpu_custom_call" | custom-call | tf_op jit(solution)/shard_map/backward/pallas_call | solution.py:513
  130.8 2.2 %settle.1 = (bf16[128,4096]{1,0:T(8,128)(2,1)}, bf16[128,1024]{1,0:T(8,128)(2,1)}, bf16[128,1024]{1,0:T(8,128)(2,1)}, f32[16,1024]{1,0:T(8,128)}) custom-call(bf16[128,4096]{1,0:T(8,128)(2,1)} %get-tuple-element.12.refs_0_, bf16[128,1024]{1,0:T(8,128)(2,1)} %get-tuple-element.13.refs_1_, bf16[128,1024]{1,0:T(8,128)(2,1)} %get-tuple-element.14.refs_2_, ...), custom_call_target="tpu_custom_call" | custom-call | tf_op jit(solution)/shard_map/settle/pallas_call | solution.py:596

commit v5 on v4

--- a/solution.py
+++ b/solution.py
@@ -448,17 +448,34 @@
         source = lax.rem(across + over, 4)
         drain(value_in.at[pl.ds(0, (8 if over else 7) * ROWS)], gather_recv.at[source])
         rows = pl.ds(pl.multiple_of(source * 8 * ROWS, 8 * ROWS), 8 * ROWS)
-        total = lax.dot_general(
-            value_in[rows, :], hidden_unit[rows, :], TN, preferred_element_type=jnp.float32
-        )
-        if over == 0:
-            summed[...] = total
+        if over != 2:
+            total = lax.dot_general(
+                value_in[rows, :], hidden_unit[rows, :], TN, preferred_element_type=jnp.float32
+            )
+            if over == 0:
+                summed[...] = total
+            else:
+                summed[...] += total
         else:
-            summed[...] += total
-    for step in RING:
-        target = lax.rem(lane + step, 8)
-        piece[target] = summed[:, columns_of(target)].astype(jnp.bfloat16)
-        send(piece.at[target], piece_in.at[lane], piece_send, piece_recv, seq=across * 8 + target)
+            for turn, part in enumerate((1 - lane // 4, lane // 4)):
+                wide = columns_of(part, 4 * ROWS)
+                summed[:, wide] += lax.dot_general(
+                    value_in[rows, :],
+                    hidden_unit[rows, wide],
+                    TN,
+                    preferred_element_type=jnp.float32,
+                )
+                for step in range(4):
+                    if turn == 0 or step:
+                        target = part * 4 + lax.rem(lane + step, 4)
+                        piece[target] = summed[:, columns_of(target)].astype(jnp.bfloat16)
+                        send(
+                            piece.at[target],
+                            piece_in.at[lane],
+                            piece_send,
+                            piece_recv,
+                            seq=across * 8 + target,
+                        )
     final[...] = summed[:, columns_of(lane)]
     drain(piece.at[pl.ds(0, 7)], piece_recv)
     total = final[...]

time: 133 us -> 132 us (level)
  no operation moved by 1% of the time
where the time goes in v5:
time: 132 us
  Pallas kernels  131 us (99%)
    pallas_call x1, Pallas kernels, backward(): pl.pallas_call(kernel, out_shape=(jax.ShapeDtypeStruct((ROWS, HEADS * HEA...  129 us

profile of v5, /device:TPU:1, one launch (start us, length us, event | category | flops | bytes accessed | tf_op | source)
XLA Modules:
  0.0 132.0 jit_solution(1429244162991808952)
XLA Ops:
  0.6 129.0 %backward.1 = (bf16[128,4096]{1,0:T(8,128)(2,1)}, bf16[128,1024]{1,0:T(8,128)(2,1)}, bf16[128,1024]{1,0:T(8,128)(2,1)}, f32[16,1024]{1,0:T(8,128)}) custom-call(bf16[128,4096]{1,0:T(8,128)(2,1)} %bitcast.12, bf16[128,4096]{1,0:T(8,128)(2,1)} %bitcast.13, bf16[128,1024]{1,0:T(8,128)(2,1)} %bitcast.16, bf16[128,1024]{1,0:T(8,128)(2,1)} %bitcast.17, ...), custom_call_target="tpu_custom_call" | custom-call | tf_op jit(solution)/shard_map/backward/pallas_call | solution.py:530
  129.7 2.2 %settle.1 = (bf16[128,4096]{1,0:T(8,128)(2,1)}, bf16[128,1024]{1,0:T(8,128)(2,1)}, bf16[128,1024]{1,0:T(8,128)(2,1)}, f32[16,1024]{1,0:T(8,128)}) custom-call(bf16[128,4096]{1,0:T(8,128)(2,1)} %get-tuple-element.12.refs_0_, bf16[128,1024]{1,0:T(8,128)(2,1)} %get-tuple-element.13.refs_1_, bf16[128,1024]{1,0:T(8,128)(2,1)} %get-tuple-element.14.refs_2_, ...), custom_call_target="tpu_custom_call" | custom-call | tf_op jit(solution)/shard_map/settle/pallas_call | solution.py:613
